TPU v7x, 256 devices: a whole 4x4x8 slice. The times are simulated.
256 devices in a mesh: tm: 8 (over x, y_hi), space: 32 (over y_lo, z, core).
Axes of the slice: x: 4, y: 4 (y_hi: 2, y_lo: 2; y = y_hi * 2 + y_lo), z: 8, core: 2. Of those that a mesh axis runs over, the one named last changes fastest.
Arguments:
- latents: bfloat16 [512, 16, 15360], P('tm', None, 'space'), may hold values from -6 to 6
- conv_kernel: bfloat16 [16, 144], replicated, may hold values from -0.5 to 0.5
- codebook: bfloat16 [16, 65536], replicated, may hold values from -6 to 6
- fine_codes: int32 [256, 15360], P('tm', 'space'), may hold values from 0 to 65535
- coarse_codes: int32 [256, 15360], P(('tm', 'space')), may hold values from 0 to 65535
Outputs:
- fine_error: bfloat16 [256, 16, 15360], P('tm', None, 'space')
- coarse_error: bfloat16 [256, 16, 15360], P(('tm', 'space'))
- code_sums: float32 [16, 65536], P(None, ('tm', 'space'))
All inputs are finite; a program needn't handle non-finite values.
Results may differ from a plain program's by a relative error of at most 0.011.
Values may be sent and summed in bfloat16 or wider, within the bound.
No kernel may reach another device: no remote copies, remote signals or barrier semaphores. Data moves between devices by JAX's collectives and lax.ppermute only.
A program may use at most 256 MiB of HBM per device.

v0:
```python
import jax
import jax.numpy as jnp
from jax import lax
from jax.sharding import PartitionSpec as P

CHANNELS = 16
CODES = 65536
WIDTH = 240


def extended_2(value, sides, width):
    for axis, dim in sides:
        size, length = (lax.axis_size(axis), value.shape[dim])
        up = [(i, (i + 1) % size) for i in range(size - 1)]
        down = [(j, i) for i, j in up]
        last = lax.slice_in_dim(value, length - width, length, axis=dim)
        first = lax.slice_in_dim(value, 0, width, axis=dim)
        before = lax.ppermute(last, axis, up)
        after = lax.ppermute(first, axis, down)
        value = jnp.concatenate([before, value, after], axis=dim)
    return value


def lift_four(frame_a, frame_b, frame_c, frame_d, position_axis):
    detail_left = (frame_b.astype(jnp.float32) - frame_a.astype(jnp.float32)).astype(jnp.bfloat16)
    smooth_left = (frame_a.astype(jnp.float32) + 0.5 * detail_left.astype(jnp.float32)).astype(
        jnp.bfloat16
    )
    detail_right = (frame_d.astype(jnp.float32) - frame_c.astype(jnp.float32)).astype(jnp.bfloat16)
    smooth_right = (frame_c.astype(jnp.float32) + 0.5 * detail_right.astype(jnp.float32)).astype(
        jnp.bfloat16
    )
    detail_top = (smooth_right.astype(jnp.float32) - smooth_left.astype(jnp.float32)).astype(
        jnp.bfloat16
    )
    smooth_top = (smooth_left.astype(jnp.float32) + 0.5 * detail_top.astype(jnp.float32)).astype(
        jnp.bfloat16
    )
    return jnp.stack([smooth_top, detail_left, detail_top, detail_right], axis=position_axis)


def shards(latents, conv_kernel, codebook, fine_codes, coarse_codes):
    half_frames = latents.shape[0] // 2
    tile_pixels = latents.shape[2]
    frame_pairs = latents.reshape(half_frames, 2, CHANNELS, tile_pixels)
    even_frames = frame_pairs[:, 0].astype(jnp.float32)
    odd_frames = frame_pairs[:, 1].astype(jnp.float32)
    detail = (odd_frames - even_frames).astype(jnp.bfloat16)
    low_band = (even_frames + 0.5 * detail.astype(jnp.float32)).astype(jnp.bfloat16)
    extended = extended_2(detail, (("space", 2),), WIDTH)
    extended = jnp.pad(extended, ((0, 0), (0, 0), (1, 1)))
    column = jnp.arange(tile_pixels) % WIDTH
    pieces = []
    for row_shift in (-1, 0, 1):
        for col_shift in (-1, 0, 1):
            offset = WIDTH + 1 + row_shift * WIDTH + col_shift
            shifted = extended[:, :, offset : offset + tile_pixels]
            if col_shift == -1:
                shifted = jnp.where(column > 0, shifted, jnp.zeros_like(shifted))
            elif col_shift == 1:
                shifted = jnp.where(column < WIDTH - 1, shifted, jnp.zeros_like(shifted))
            pieces.append(shifted)
    stacked = jnp.concatenate(pieces, axis=1)
    encoded = detail.astype(jnp.float32) + jnp.einsum(
        "ok,fkp->fop", conv_kernel, stacked, preferred_element_type=jnp.float32
    )
    looked = jnp.moveaxis(jnp.take(codebook, fine_codes, axis=1), 0, 1).astype(jnp.float32)
    fine_error = (encoded - looked).astype(jnp.bfloat16)
    code_totals = jnp.zeros((CHANNELS, CODES), jnp.float32)
    code_totals = code_totals.at[:, fine_codes.reshape(-1)].add(
        jnp.moveaxis(encoded, 0, 1).reshape(CHANNELS, -1)
    )
    groups = low_band.reshape(half_frames // 4, 4, CHANNELS, tile_pixels)
    lifted = lift_four(groups[:, 0], groups[:, 1], groups[:, 2], groups[:, 3], 1)
    lifted = lifted.reshape(half_frames, CHANNELS, tile_pixels)
    coarse = lax.all_to_all(lifted, "space", split_axis=0, concat_axis=2, tiled=True)
    coarse_values = coarse.astype(jnp.float32)
    coarse_looked = jnp.moveaxis(jnp.take(codebook, coarse_codes, axis=1), 0, 1).astype(jnp.float32)
    coarse_error = (coarse_values - coarse_looked).astype(jnp.bfloat16)
    code_totals = code_totals.at[:, coarse_codes.reshape(-1)].add(
        jnp.moveaxis(coarse_values, 0, 1).reshape(CHANNELS, -1)
    )
    all_totals = lax.psum(code_totals, ("tm", "space"))
    share_rows = CODES // lax.axis_size(("tm", "space"))
    code_sums = lax.dynamic_slice_in_dim(
        all_totals, lax.axis_index(("tm", "space")) * share_rows, share_rows, 1
    )
    return (fine_error, coarse_error, code_sums)


def solution(mesh):
    placed = (P("tm", None, "space"), P(), P(), P("tm", "space"), P(("tm", "space"), None))
    return jax.shard_map(
        shards,
        mesh=mesh,
        in_specs=placed,
        out_specs=(
            P("tm", None, "space"),
            P(("tm", "space"), None, None),
            P(None, ("tm", "space")),
        ),
        check_vma=False,
    )
```

profile of v0, /device:TPU:2, one launch (start us, length us, event | category | flops | bytes accessed | tf_op | source)
XLA Modules:
  0.0 810.5 jit_solution(10540734188070157060)
XLA Ops:
  7.2 1.4 fusion.22
  8.6 0.8 fusion.45
  9.4 1.4 collective-permute-start.1
  10.8 3.0 collective-permute-start
  13.8 1.5 fusion.29
  15.8 0.9 pad_maximum_fusion.2
  16.7 10.5 %all-to-all-start = ((bf16[32,16,480]{2,1,0:T(8,128)(2,1)}), bf16[32,16,480]{2,1,0:T(8,128)(2,1)S(1)}, u32[]{:S(2)}, u32[]{:S(2)}) async-start(bf16[32,16,480]{2,1,0:T(8,128)(2,1)} %bitcast.8), calls=%async_computation | async-start | bytes 1048576 | tf_op jit(solution)/shard_map/all_to_all | solution.py:76
  27.4 0.9 and_reduce_fusion
  28.5 0.6 broadcast_clamp_fusion
  29.1 0.7 compare_select_fusion.1
  29.8 12.4 %copy.37 = bf16[16,65536]{0,1:T(8,128)(2,1)} copy(bf16[16,65536]{1,0:T(8,128)(2,1)} %param.7) | data formatting | bytes 4194304 | tf_op args[2]
  42.2 60.0 %gather_fusion = bf16[15360,16]{1,0:T(8,128)(2,1)} fusion(bf16[16,65536]{0,1:T(8,128)(2,1)} %copy.37, s32[15360]{0:T(1024)S(1)} %broadcast_clamp_fusion.1), kind=kCustom, calls=%fused_computation | custom fusion | bytes 1044480 | tf_op jit(solution)/shard_map/jit(_take)/gather | solution.py:67
  102.2 3.6 copy.39
  105.8 65.0 %gather_fusion.1 = bf16[15360,16]{1,0:T(8,128)(2,1)} fusion(bf16[16,65536]{0,1:T(8,128)(2,1)} %copy.37, s32[15360]{0:T(1024)} %broadcast_clamp_fusion), kind=kCustom, calls=%fused_computation.1 | custom fusion | bytes 1044480 | tf_op jit(solution)/shard_map/jit(_take)/gather | solution.py:78
  170.8 0.6 fusion.9
  172.1 0.3 fusion.26
  173.9 1.6 fusion.10
  175.4 0.6 copy.42
  176.1 0.6 reshape.203
  176.7 4.5 copy.43
  181.2 95.3 %scatter_custom_fusion = f32[16,65536]{0,1:T(8,128)} fusion(s32[15360]{0:T(1024)} %bitcast.75, f32[15360,16]{1,0:T(8,128)} %copy.43, f32[]{:T(128)} %constant.39.clone.1), kind=kCustom, calls=%fused_computation.4 | custom fusion | flops 245760 | bytes 4194816 | tf_op jit(solution)/shard_map/scatter-add | solution.py:70
  276.6 4.7 copy.40
  281.3 0.6 copy.44
  281.9 0.6 reshape.211
  282.5 4.5 copy.45
  287.0 95.5 %scatter_fusion = f32[16,65536]{0,1:T(8,128)} fusion(f32[16,65536]{0,1:T(8,128)} %scatter_custom_fusion, s32[15360]{0:T(1024)S(1)} %bitcast.73, f32[15360,16]{1,0:T(8,128)} %copy.45), kind=kCustom, calls=%fused_computation.3 | custom fusion | flops 245760 | bytes 3010560 | tf_op jit(solution)/shard_map/scatter-add | solution.py:80
  382.5 0.7 copy-done.5
  383.2 10.0 %fusion.2 = bf16[1,16,15360]{1,2,0:T(8,128)(2,1)} fusion(f32[1,16,32,480]{1,3,2,0:T(8,128)} %copy.40, bf16[15360,16]{1,0:T(8,128)(2,1)} %gather_fusion.1, pred[15360]{0:T(1024)(128)(4,1)S(1)} %copy-done.5), kind=kLoop, calls=%fused_computation.7 | loop fusion | flops 983040 | bytes 1981440 | tf_op jit(solution)/shard_map/convert_element_type | solution.py:79
  393.2 4.3 copy.46
  397.5 404.5 %all-reduce.3.cloned.1.call-done = f32[16,65536]{0,1:T(8,128)} async-done(((f32[16,65536]{0,1:T(8,128)}), f32[16,65536]{0,1:T(8,128)}) %all-reduce.3.cloned.1.call-update) | async-done | bytes 4194320 | tf_op jit(solution)/shard_map/psum | solution.py:83
  802.0 0.9 constant_dynamic-slice_fusion
  802.9 0.7 copy.47
  (35 shorter events, 3.0 us)
Async XLA Ops:
  7.2 166.7 %copy-start = (bf16[16,144]{1,0:T(8,128)(2,1)S(1)}, bf16[16,144]{1,0:T(8,128)(2,1)}, u32[]{:S(2)}) copy-start(bf16[16,144]{1,0:T(8,128)(2,1)} %param.6) | copy-start | bytes 13828
  9.4 17.9 %copy-start.3 = (s32[32,480]{1,0:T(8,128)S(1)}, s32[32,480]{1,0:T(8,128)}, u32[]{:S(2)}) copy-start(s32[32,480]{1,0:T(8,128)} %param.8) | copy-start | bytes 184324
  9.4 18.1 %copy-start.4 = (s32[1,15360]{1,0:T(1,128)S(1)}, s32[1,15360]{1,0:T(1,128)}, u32[]{:S(2)}) copy-start(s32[1,15360]{1,0:T(1,128)} %param.9) | copy-start | bytes 184324
  9.4 161.4 %collective-permute-start.1 = (bf16[32,16,240]{2,1,0:T(8,128)(2,1)}, bf16[32,16,240]{2,1,0:T(8,128)(2,1)S(1)}, u32[]{:S(2)}, u32[]{:S(2)}) collective-permute-start(bf16[32,16,240]{2,1,0:T(8,128)(2,1)} %get-tuple-element.24), channel_id=1, source_target_pairs={{1,0},{2,1},{3,2},{4,3},{5,4},{6,5},{7,6},{8,7},{9,8},{10,9},{11,1... | collective-permute-start | bytes 737288 | tf_op jit(solution)/shard_map/ppermute | solution.py:19
  10.8 160.0 %collective-permute-start = (bf16[32,16,240]{2,1,0:T(8,128)(2,1)S(1)}, bf16[32,16,240]{2,1,0:T(8,128)(2,1)S(1)}, u32[]{:S(2)}, u32[]{:S(2)}) collective-permute-start(bf16[32,16,240]{2,1,0:T(8,128)(2,1)S(1)} %get-tuple-element.23), channel_id=1, source_target_pairs={{0,1},{1,2},{2,3},{3,4},{4,5},{5,6},{6,7},{7,8},{8,9},{9,10},{10,1... | collective-permute-start | bytes 737288 | tf_op jit(solution)/shard_map/ppermute | solution.py:18
  16.7 259.8 %all-to-all-start = ((bf16[32,16,480]{2,1,0:T(8,128)(2,1)}), bf16[32,16,480]{2,1,0:T(8,128)(2,1)S(1)}, u32[]{:S(2)}, u32[]{:S(2)}) async-start(bf16[32,16,480]{2,1,0:T(8,128)(2,1)} %bitcast.8), calls=%async_computation | async-start | bytes 1048576 | tf_op jit(solution)/shard_map/all_to_all | solution.py:76
  27.2 774.8 %all-reduce.3.cloned.1.call-start = ((), (), s32[]{:S(2)}) async-start(), calls=%async_computation.1 | async-start | bytes 67108864 | tf_op jit(solution)/shard_map/psum | solution.py:83
  105.8 66.7 %copy-start.2 = (bf16[64,16,480]{2,1,0:T(8,128)(2,1)S(1)}, bf16[64,16,480]{2,1,0:T(8,128)(2,1)}, u32[]{:S(2)}) copy-start(bf16[64,16,480]{2,1,0:T(8,128)(2,1)} %param.5) | copy-start | bytes 2949124
  382.5 0.7 copy-start.5
  383.2 420.4 %copy-start.1 = (bf16[16,144]{1,0:T(8,128)(2,1)S(1)}, bf16[16,144]{1,0:T(8,128)(2,1)}, u32[]{:S(2)}) copy-start(bf16[16,144]{1,0:T(8,128)(2,1)} %param.6) | copy-start | bytes 13828
Sparse Core Ops, SparseCore 0:
  382.6 419.3 all-reduce.2
where the time goes:
time: 813 us; the launch traced here: 810 us
  waiting for transfers between devices  405 us (50%)
  other arithmetic  210 us (26%)
  local copies, waits for them, and re-layouts  165 us (20%)
  starting transfers between devices  15 us (2%)
  between operations  14.3 us (2%)
    psum x1, waiting for transfers between devices, shards(): all_totals = lax.psum(code_totals, ('tm', 'space'))  404 us
    scatter-add x1, other arithmetic, shards(): code_totals.at[:, coarse_codes.reshape(-1)]  95.5 us
    scatter-add x1, other arithmetic, shards(): code_totals.at[:, fine_codes.reshape(-1)]  95.3 us
    gather x1, local copies, waits for them, and re-layouts, shards(): jnp.take(codebook, coarse_codes, axis=1)  65 us
    gather x2, local copies, waits for them, and re-layouts, shards(): jnp.take(codebook, fine_codes, axis=1)  63.5 us
    unnamed x15, local copies, waits for them, and re-layouts  18.1 us
  transfers between devices with their start and end apart: 4, of which 1 were waited for; matrix products, arithmetic and copies ran while one was open for 33% of the time, Pallas kernels for 0%

commit v1 on v0

v1 whole, which is shorter than its diff:
```python
import functools

import jax
import jax.numpy as jnp
import numpy as np
from jax import lax
from jax.experimental import pallas as pl
from jax.experimental.pallas import tpu as pltpu
from jax.sharding import Mesh, PartitionSpec as P

CHANNELS = 16
CODES = 65536
WIDTH = 240
TILE = 480
ROW = 256
LINE = 512
LINES = 32
ROWS = CODES // 4
TABLES = 4
MIB = 2**20
f32, bf16 = jnp.float32, jnp.bfloat16

SPACE = ("yl", "z", "core")
FRAMES_BY = ("x", "yh")
Y = ("yh", "yl")
CORES = ("x", "yh", "yl", "z", "core")

VMEM = pl.BlockSpec(memory_space=pltpu.VMEM)
HBM = pl.BlockSpec(memory_space=pl.ANY)


def nt(a, b):
    return lax.dot_general(a, b, (((1,), (1,)), ((), ())), preferred_element_type=f32)


def lift_kernel(lat_ref, head_ref, tail_ref, lifted_ref):
    gap = jnp.zeros((CHANNELS, ROW - WIDTH), f32)

    def group(g, carry):
        low = []
        for k in range(4):
            even = lat_ref[8 * g + 2 * k].astype(f32)
            odd = lat_ref[8 * g + 2 * k + 1].astype(f32)
            wide = (odd - even).astype(bf16).astype(f32)
            head_ref[4 * g + k] = jnp.concatenate([wide[:, :WIDTH], gap], axis=1).astype(bf16)
            tail_ref[4 * g + k] = jnp.concatenate([wide[:, WIDTH:], gap], axis=1).astype(bf16)
            low.append((even + 0.5 * wide).astype(bf16).astype(f32))
        a, b, c, d = low
        left = (b - a).astype(bf16)
        smooth_left = (a + 0.5 * left.astype(f32)).astype(bf16).astype(f32)
        right = (d - c).astype(bf16)
        smooth_right = (c + 0.5 * right.astype(f32)).astype(bf16).astype(f32)
        top = (smooth_right - smooth_left).astype(bf16)
        lifted_ref[4 * g] = (smooth_left + 0.5 * top.astype(f32)).astype(bf16)
        lifted_ref[4 * g + 1] = left
        lifted_ref[4 * g + 2] = top
        lifted_ref[4 * g + 3] = right
        return carry

    for g in range(lat_ref.shape[0] // 8):
        group(g, 0)


def lift(latents):
    half = latents.shape[0] // 2
    shape = jax.ShapeDtypeStruct((half, CHANNELS, TILE), bf16)
    edge = jax.ShapeDtypeStruct((half, CHANNELS, ROW), bf16)
    return pl.pallas_call(
        lift_kernel,
        out_shape=[edge, edge, shape],
        grid=(4,),
        in_specs=[pl.BlockSpec((half // 2, CHANNELS, TILE), lambda i: (i, 0, 0))],
        out_specs=[pl.BlockSpec((half // 4, CHANNELS, n), lambda i: (i, 0, 0)) for n in (ROW, ROW, TILE)],
        name="lift",
        compiler_params=pltpu.CompilerParams(vmem_limit_bytes=60 * MIB),
    )(latents)


def identity():
    return jnp.asarray(np.eye(256), bf16)


def table_kernel(codebook_ref, eye_ref, table_ref):
    blank = jnp.zeros((16, 256), bf16)
    for k in range(4):
        pieces = []
        for h in range(2):
            start = pl.multiple_of(pl.program_id(0) * 2048 + k * 512 + h * 256, 256)
            for s in range(4):
                pieces += [codebook_ref[:, pl.ds(s * ROWS + start, 256)], blank]
        block = nt(eye_ref[...], jnp.concatenate(pieces, axis=0))
        table_ref[k * 512 : k * 512 + 256, :] = block[:, :128]
        table_ref[k * 512 + 256 : k * 512 + 512, :] = block[:, 128:]


def code_table(codebook):
    return pl.pallas_call(
        table_kernel,
        grid=(ROWS // 2048,),
        out_shape=jax.ShapeDtypeStruct((ROWS, 128), f32),
        in_specs=[pl.BlockSpec((CHANNELS, CODES), lambda i: (0, 0)), pl.BlockSpec((256, 256), lambda i: (0, 0))],
        out_specs=pl.BlockSpec((2048, 128), lambda i: (i, 0)),
        name="code_table",
        compiler_params=pltpu.CompilerParams(vmem_limit_bytes=60 * MIB),
        cost_estimate=pl.CostEstimate(flops=10**9, bytes_accessed=10**7, transcendentals=0),
    )(codebook, identity())


def pick_matrix(offset):
    m = np.zeros((64, 128), np.float32)
    for slot in range(4):
        for c in range(16):
            m[slot * 16 + c, slot * 32 + offset + c] = 1.0
    return jnp.asarray(m, bf16)


def put_rows(codes, rows_ref, smem, sem):
    rows_ref[...] = codes & (ROWS - 1)
    copies = [pltpu.make_async_copy(rows_ref.at[u], smem[u], sem.at[u]) for u in range(LINES)]
    for c in copies:
        c.start()
    return copies


def slotted(values, codes_line):
    slot = codes_line >> 14
    blank = jnp.zeros((16, LINE), f32)
    pieces = []
    for s in range(4):
        pieces += [blank, jnp.where(slot == s, values, 0.0)]
    return jnp.concatenate(pieces, axis=0).astype(bf16)


def place_pair(first, second, eye, vals_ref, u):
    for h in range(2):
        at = slice(256 * h, 256 * h + 256)
        block = nt(eye, jnp.concatenate([first[:, at], second[:, at]], axis=0))
        for k in range(2):
            start = pl.multiple_of((u + k) * LINE + 256 * h, 256)
            vals_ref[pl.ds(start, 256), :] = block[:, 128 * k : 128 * k + 128]


def looked_up(vals_ref, codes_line, pick, u):
    start = pl.multiple_of(u * LINE, LINE)
    rows = vals_ref[pl.ds(start, LINE), :].astype(bf16)
    parts = nt(pick, rows)
    slot = codes_line >> 14
    out = parts[:16]
    for s in range(1, 4):
        out = jnp.where(slot == s, parts[s * 16 : (s + 1) * 16], out)
    return out


def walk(smem, vals_ref, tables, start, stop):
    def step(g, carry):
        for base in range(0, LINES, TABLES):
            at = [smem[base + t][g] for t in range(TABLES)]
            rows = [tables[t][pl.ds(at[t], 1), :] for t in range(TABLES)]
            adds = [vals_ref[pl.ds((base + t) * LINE + g, 1), :] for t in range(TABLES)]
            for t in range(TABLES):
                vals_ref[pl.ds((base + t) * LINE + g, 1), :] = rows[t]
                tables[t][pl.ds(at[t], 1), :] = rows[t] + adds[t]
        return carry

    lax.fori_loop(start, stop, step, 0)


def quantize_kernel(before_ref, head_ref, tail_ref, after_ref, values_ref, weights_ref, fine_codes_ref, coarse_codes_ref,
                    eye_ref, pick_ref, pick_sum_ref, table_in, fine_error_ref, coarse_error_ref, keep_ref, send_ref,
                    t0, t1, t2, t3, vals_ref, enc_ref, fine_padded, coarse_padded, fine_rows, coarse_rows, *rest):
    fine_smem, coarse_smem, (fine_sem, coarse_sem, in_sem) = rest[:LINES], rest[LINES : 2 * LINES], rest[2 * LINES :]
    tables = [t0, t1, t2, t3]
    fetch = pltpu.make_async_copy(table_in, t0, in_sem)
    fetch.start()
    gap = jnp.zeros((LINES, ROW - WIDTH), jnp.int32)
    fine_padded[...] = jnp.concatenate([fine_codes_ref[:, :WIDTH], gap, fine_codes_ref[:, WIDTH:], gap], axis=1)
    fine_copies = put_rows(fine_padded[...], fine_rows, fine_smem, fine_sem)
    gap = jnp.zeros((1, LINE - TILE), jnp.int32)
    for u in range(LINES):
        coarse_padded[u : u + 1, :] = jnp.concatenate([coarse_codes_ref[:, u * TILE : (u + 1) * TILE], gap], axis=1)
    coarse_copies = put_rows(coarse_padded[...], coarse_rows, coarse_smem, coarse_sem)
    weights, eye, pick, pick_sum = weights_ref[...], eye_ref[...], pick_ref[...], pick_sum_ref[...]

    def encoded(u):
        lines = [r[u].astype(f32) for r in (before_ref, head_ref, tail_ref, after_ref)]
        moved = [[pltpu.roll(v, 1, 1) for v in lines], lines, [pltpu.roll(v, ROW - 1, 1) for v in lines]]
        pieces = []
        for r in range(3):
            for m in moved:
                pieces.append(jnp.concatenate([m[r], m[r + 1]], axis=1).astype(bf16))
        stacked = jnp.concatenate(pieces, axis=0)
        enc = jnp.concatenate([lines[1], lines[2]], axis=1) + jnp.dot(weights, stacked, preferred_element_type=f32)
        enc_ref[u] = enc
        return slotted(enc, fine_padded[pl.ds(u, 1), :])

    def encode(p, carry):
        for k in range(2):
            u = 4 * p + 2 * k
            place_pair(encoded(u), encoded(u + 1), eye, vals_ref, u)
        return carry

    lax.fori_loop(0, LINES // 4, encode, 0)
    fetch.wait()

    def spread(i, carry):
        at = pl.ds(pl.multiple_of(i * 64, 64), 64)
        code_part = t0[at, :]
        for t in tables[1:]:
            t[at, :] = code_part
        return carry

    lax.fori_loop(0, ROWS // 64, spread, 0)
    for c in fine_copies:
        c.wait()
    walk(fine_smem, vals_ref, tables, 0, WIDTH)
    walk(fine_smem, vals_ref, tables, ROW, ROW + WIDTH)

    tail_gap = jnp.zeros((CHANNELS, LINE - TILE), f32)

    def slots_of(u):
        values = jnp.concatenate([values_ref[u].astype(f32), tail_gap], axis=1)
        return slotted(values, coarse_padded[pl.ds(u, 1), :])

    def turn(p, carry):
        for k in range(4):
            u = 4 * p + k
            error = enc_ref[u] - looked_up(vals_ref, fine_padded[pl.ds(u, 1), :], pick, u)
            fine_error_ref[u] = jnp.concatenate([error[:, :WIDTH], error[:, ROW : ROW + WIDTH]], axis=1).astype(bf16)
        for k in range(2):
            u = 4 * p + 2 * k
            place_pair(slots_of(u), slots_of(u + 1), eye, vals_ref, u)
        return carry

    lax.fori_loop(0, LINES // 4, turn, 0)
    for c in coarse_copies:
        c.wait()
    walk(coarse_smem, vals_ref, tables, 0, TILE)
    my_x, my_y, my_z, my_core = (lax.axis_index(a) for a in ("x", Y, "z", "core"))

    def total(i, carry):
        for out_ref, core in ((send_ref, 1 - my_core), (keep_ref, my_core)):
            b = 2 * i + core
            at = pl.ds(pl.multiple_of(b * 256, 256), 256)
            summed = t0[at, :] + t1[at, :] + t2[at, :] + t3[at, :]
            parts = nt(pick_sum, summed.astype(bf16)).astype(bf16)
            y_off = ((b >> 4) - my_y) & 3
            z_off = ((b >> 1) & 7) ^ my_z
            z_top = z_off >> 2
            z_at = z_off ^ (3 * z_top)
            for s in range(4):
                x_off = (s - my_x) & 3
                place = (jnp.where(core == 0, x_off, y_off), jnp.where(core == 0, y_off, x_off), z_at)
                out_ref[place] = parts[s * 16 : (s + 1) * 16]
        return carry

    lax.fori_loop(0, ROWS // 512, total, 0)
    for q in range(LINES // 4):
        parts = []
        for k in range(4):
            u = 4 * q + k
            looked = looked_up(vals_ref, coarse_padded[u : u + 1, :], pick, u)
            parts.append(values_ref[u].astype(f32) - looked[:, :TILE])
        coarse_error_ref[0, :, q * 4 * TILE : (q + 1) * 4 * TILE] = jnp.concatenate(parts, axis=1).astype(bf16)


def quantize(before, head, tail, after, values, weights, fine_codes, coarse_codes, table):
    sums = jax.ShapeDtypeStruct((4, 4, 8, CHANNELS, 256), bf16)
    return pl.pallas_call(
        quantize_kernel,
        out_shape=[jax.ShapeDtypeStruct((LINES, CHANNELS, TILE), bf16),
                   jax.ShapeDtypeStruct((1, CHANNELS, LINES * TILE), bf16), sums, sums],
        in_specs=[VMEM] * 11 + [HBM],
        out_specs=[VMEM] * 4,
        scratch_shapes=[pltpu.VMEM((ROWS, 128), f32)] * TABLES
        + [pltpu.VMEM((LINES * LINE, 128), f32), pltpu.VMEM((LINES, CHANNELS, LINE), f32)]
        + [pltpu.VMEM((LINES, LINE), jnp.int32)] * 4
        + [pltpu.SMEM((LINE,), jnp.int32)] * (2 * LINES)
        + [pltpu.SemaphoreType.DMA((LINES,)), pltpu.SemaphoreType.DMA((LINES,)), pltpu.SemaphoreType.DMA],
        name="quantize",
        compiler_params=pltpu.CompilerParams(vmem_limit_bytes=58 * MIB),
        cost_estimate=pl.CostEstimate(flops=10**9, bytes_accessed=10**8, transcendentals=0),
    )(before, head, tail, after, values, weights, fine_codes, coarse_codes, identity(), pick_matrix(0), pick_matrix(16), table)


def device_of(x, y, z, core):
    return ((x % 4 * 4 + y % 4) * 8 + z) * 2 + core


def permuted(value, target):
    pairs = [(device_of(x, y, z, c), device_of(*target(x, y, z, c)))
             for x in range(4) for y in range(4) for z in range(8) for c in range(2)]
    return lax.ppermute(value, CORES, pairs)


def along(first, k):
    def target(x, y, z, c):
        return (x + k, y, z, c) if (c == 0) == first else (x, y + k, z, c)
    return target


def across(bits):
    return lambda x, y, z, c: (x, y, z ^ bits, c)


def add_kernel(n_in, *refs):
    ins, outs = refs[:n_in], refs[n_in:]
    rows = ins[0].shape[0] // len(outs)

    def piece(k, i):
        total = ins[0][k * rows + i].astype(f32)
        for r in ins[1:]:
            total = total + r[k * rows + i].astype(f32)
        outs[k][i] = total.astype(outs[k].dtype)

    for k in range(len(outs)):
        if rows <= 4:
            for i in range(rows):
                piece(k, i)
        else:
            def several(j, carry, k=k):
                for i in range(4):
                    piece(k, 4 * j + i)
                return carry
            lax.fori_loop(0, rows // 4, several, 0)


def added(ways, *parts):
    share = parts[0].shape[0] // ways
    shapes = [jax.ShapeDtypeStruct((share, CHANNELS, 256), f32 if k == 0 else bf16) for k in range(ways)]
    return pl.pallas_call(
        functools.partial(add_kernel, len(parts)),
        out_shape=shapes,
        in_specs=[VMEM] * len(parts),
        out_specs=[VMEM] * ways,
        name="add",
        compiler_params=pltpu.CompilerParams(vmem_limit_bytes=16 * MIB),
    )(*parts)


def shared_sums(keep, send):
    keep, send = (v.reshape(128, CHANNELS, 256) for v in (keep, send))
    own, *sends = added(4, keep, permuted(send, lambda x, y, z, c: (x, y, z, 1 - c)))
    for first in (True, False):
        got = [permuted(s, along(first, k + 1)) for k, s in enumerate(sends)]
        own, *sends = added(4 if first else 2, own, *got)
    for bits, ways in ((7, 2), (2, 2), (1, 1)):
        own, *sends = added(ways, own, permuted(sends[0], across(bits)))
    return own[0]


def shards(latents, conv_kernel, codebook, fine_codes, coarse_codes):
    head, tail, lifted = lift(latents)
    size = lax.axis_size(SPACE)
    up = [(i, i + 1) for i in range(size - 1)]
    before = lax.ppermute(tail, SPACE, up)
    after = lax.ppermute(head, SPACE, [(j, i) for i, j in up])
    table = code_table(codebook)
    moved = lax.all_to_all(lifted, SPACE, split_axis=0, concat_axis=0, tiled=True)
    fine_error, coarse_error, keep, send = quantize(
        before, head, tail, after, moved, conv_kernel, fine_codes, coarse_codes, table)
    return fine_error, coarse_error, shared_sums(keep, send)


def solution(mesh):
    split = Mesh(mesh.devices.reshape(4, 2, 2, 8, 2), CORES)
    return jax.shard_map(
        shards,
        mesh=split,
        in_specs=(P(FRAMES_BY, None, SPACE), P(), P(), P(FRAMES_BY, SPACE), P(CORES, None)),
        out_specs=(P(FRAMES_BY, None, SPACE), P(CORES, None, None), P(None, CORES)),
        check_vma=False,
    )
```

time: 813 us -> 136 us (0.17)
  waiting for transfers between devices: 405 us -> 30.1 us
  other arithmetic: 210 us -> 0 us
  local copies, waits for them, and re-layouts: 165 us -> 2.04 us
  Pallas kernels: 0 us -> 74.5 us
  starting transfers between devices: 15 us -> 28.8 us
  between operations: 14.3 us -> 0.72 us
    psum x1 -> x0, waiting for transfers between devices: 404 us -> none  [shards(): all_totals = lax.psum(code_totals, ('tm', 'space'))]
    scatter-add x2 -> x0, other arithmetic: 191 us -> none  [the longest x1 95.5 us: shards(): code_totals.at[:, coarse_codes.reshape(-1)]]
    gather x3 -> x0, local copies, waits for them, and re-layouts: 129 us -> none  [the longest x1 65 us: shards(): jnp.take(codebook, coarse_codes, axis=1)]
    pallas_call x0 -> x9, Pallas kernels: none -> 74.5 us  [the longest x1 62.3 us: quantize(): pl.pallas_call(quantize_kernel, out_shape=[jax.ShapeDtypeStruct((LINES, C...]
    ppermute x2 -> x12, waiting for transfers between devices: 0.01 us -> 22.5 us  [the longest x10 22.5 us: permuted(): return lax.ppermute(value, CORES, pairs)]
    unnamed x15 -> x8, local copies, waits for them, and re-layouts: 18.1 us -> 2.04 us
    ppermute x2 -> x12, starting transfers between devices: 4.46 us -> 18.9 us  [the longest x10 15.4 us: permuted(): return lax.ppermute(value, CORES, pairs)]
    convert_element_type x6 -> x0, other arithmetic: 13.4 us -> none  [the longest x1 9.99 us: shards(): coarse_error = (coarse_values - coarse_looked).astype(jnp.bfloat16)]
  transfers between devices with their start and end apart: 4 -> 13, of which waited for: 1 -> 11; matrix products, arithmetic and copies ran while one was open for 33% -> 0% of each run, Pallas kernels for 0% -> 5%
where the time goes in v1:
time: 136 us
  Pallas kernels  74.5 us (55%)
  waiting for transfers between devices  30.1 us (22%)
  starting transfers between devices  28.8 us (21%)
  local copies, waits for them, and re-layouts  2.04 us (2%)
    pallas_call x1, Pallas kernels, quantize(): pl.pallas_call(quantize_kernel, out_shape=[jax.ShapeDtypeStruct((LINES, C...  62.3 us
    ppermute x10, waiting for transfers between devices, permuted(): return lax.ppermute(value, CORES, pairs)  22.5 us
    ppermute x10, starting transfers between devices, permuted(): return lax.ppermute(value, CORES, pairs)  15.4 us
    all_to_all x1, starting transfers between devices, shards(): lax.all_to_all(lifted, SPACE, split_axis=0, concat_axis=0, tiled=True)  9.87 us
    all_to_all x1, waiting for transfers between devices, shards(): lax.all_to_all(lifted, SPACE, split_axis=0, concat_axis=0, tiled=True)  7.59 us
    pallas_call x1, Pallas kernels, code_table(): pl.pallas_call(table_kernel, grid=(ROWS // 2048,), out_shape=jax.ShapeDty...  7.34 us
    pallas_call x1, Pallas kernels, lift(): pl.pallas_call(lift_kernel, out_shape=[edge, edge, shape], grid=(4,), in_...  3.63 us
  transfers between devices with their start and end apart: 13, of which 11 were waited for; matrix products, arithmetic and copies ran while one was open for 0% of the time, Pallas kernels for 5%

profile of v1, /device:TPU:2, one launch (start us, length us, event | category | flops | bytes accessed | tf_op | source)
XLA Modules:
  0.0 136.1 jit_solution(12861810309295597111)
XLA Ops:
  0.6 3.6 %lift.1 = (bf16[32,16,256]{2,1,0:T(8,128)(2,1)}, bf16[32,16,256]{2,1,0:T(8,128)(2,1)}, bf16[32,16,480]{2,1,0:T(8,128)(2,1)}) custom-call(bf16[64,16,480]{2,1,0:T(8,128)(2,1)} %lat_ref.1), custom_call_target="tpu_custom_call" | custom-call | tf_op jit(solution)/shard_map/lift/pallas_call | solution.py:68
  4.3 9.9 %all-to-all-start = ((bf16[32,16,480]{2,1,0:T(8,128)(2,1)}), bf16[32,16,480]{2,1,0:T(8,128)(2,1)S(1)}, u32[]{:S(2)}, u32[]{:S(2)}) async-start(bf16[32,16,480]{2,1,0:T(8,128)(2,1)} %get-tuple-element.26), calls=%async_computation | async-start | bytes 1048576 | tf_op jit(solution)/shard_map/all_to_all | solution.py:358
  14.1 2.2 %collective-permute-start = (bf16[32,16,256]{2,1,0:T(8,128)(2,1)}, bf16[32,16,256]{2,1,0:T(8,128)(2,1)S(1)}, u32[]{:S(2)}, u32[]{:S(2)}) collective-permute-start(bf16[32,16,256]{2,1,0:T(8,128)(2,1)} %get-tuple-element.24.tail_ref), channel_id=1, source_target_pairs={{0,1},{1,2},{2,3},{3,4},{4,5},{5,6},{6,7},{7,8},{8,9},{9,10},{10,1... | collective-permute-start | bytes 786440 | tf_op jit(solution)/shard_map/ppermute | solution.py:355
  16.3 1.3 collective-permute-start.1
  17.6 7.3 %code_table.1.table_in = f32[16384,128]{1,0:T(8,128)} custom-call(bf16[16,65536]{1,0:T(8,128)(2,1)} %codebook_ref.1, bf16[256,256]{1,0:T(8,128)(2,1)} %constant.6.clone.eye_ref), custom_call_target="tpu_custom_call" | custom-call | flops 1000000000 | bytes 10000000 | tf_op jit(solution)/shard_map/code_table/pallas_call | solution.py:97
  25.0 7.6 %all-to-all-done.values_ref = bf16[32,16,480]{2,1,0:T(8,128)(2,1)S(1)} async-done(((bf16[32,16,480]{2,1,0:T(8,128)(2,1)}), bf16[32,16,480]{2,1,0:T(8,128)(2,1)S(1)}, u32[]{:S(2)}, u32[]{:S(2)}) %all-to-all-start) | async-done | bytes 491552 | tf_op jit(solution)/shard_map/all_to_all | solution.py:358
  32.6 0.8 copy-done.1
  33.4 62.3 %quantize.1 = (bf16[32,16,480]{2,1,0:T(8,128)(2,1)}, bf16[1,16,15360]{2,1,0:T(8,128)(2,1)}, bf16[4,4,8,16,256]{4,3,2,1,0:T(8,128)(2,1)}, bf16[4,4,8,16,256]{4,3,2,1,0:T(8,128)(2,1)}) custom-call(bf16[32,16,256]{2,1,0:T(8,128)(2,1)} %copy-done.2, bf16[32,16,256]{2,1,0:T(8,128)(2,1)} %get-tuple-element.25.head_ref, ...), custom_call_target="tpu_custom_call" | custom-call | flops 1000000000 | bytes 100000000 | tf_op jit(solution)/shard_map/quantize/pallas_call | solution.py:268
  95.7 0.1 collective-permute-start.2
  95.8 2.9 %collective-permute-done.2.refs_1_ = bf16[128,16,256]{2,1,0:T(8,128)(2,1)S(1)} collective-permute-done((bf16[128,16,256]{2,1,0:T(8,128)(2,1)}, bf16[128,16,256]{2,1,0:T(8,128)(2,1)S(1)}, u32[]{:S(2)}, u32[]{:S(2)}) %collective-permute-start.2) | collective-permute-done | bytes 1048608 | tf_op jit(solution)/shard_map/ppermute | solution.py:292
  98.7 1.2 copy-done
  99.9 0.4 add.6
  100.3 1.6 %collective-permute-start.3 = (bf16[32,16,256]{2,1,0:T(8,128)(2,1)S(1)}, bf16[32,16,256]{2,1,0:T(8,128)(2,1)S(1)}, u32[]{:S(2)}, u32[]{:S(2)}) collective-permute-start(bf16[32,16,256]{2,1,0:T(8,128)(2,1)S(1)} %get-tuple-element.32), channel_id=1, source_target_pairs={{0,64},{1,17},{2,66},{3,19},{4,68},{5,21},{6,70},{7,23},{8,72},{9,... | collective-permute-start | bytes 786440 | tf_op jit(solution)/shard_map/ppermute | solution.py:292
  101.9 1.1 collective-permute-start.4
  103.0 2.1 %collective-permute-start.5 = (bf16[32,16,256]{2,1,0:T(8,128)(2,1)S(1)}, bf16[32,16,256]{2,1,0:T(8,128)(2,1)S(1)}, u32[]{:S(2)}, u32[]{:S(2)}) collective-permute-start(bf16[32,16,256]{2,1,0:T(8,128)(2,1)S(1)} %get-tuple-element.34), channel_id=1, source_target_pairs={{0,192},{1,49},{2,194},{3,51},{4,196},{5,53},{6,198},{7,55},{8,200... | collective-permute-start | bytes 786440 | tf_op jit(solution)/shard_map/ppermute | solution.py:292
  105.1 1.6 %collective-permute-done.3.refs_1_ = bf16[32,16,256]{2,1,0:T(8,128)(2,1)S(1)} collective-permute-done((bf16[32,16,256]{2,1,0:T(8,128)(2,1)S(1)}, bf16[32,16,256]{2,1,0:T(8,128)(2,1)S(1)}, u32[]{:S(2)}, u32[]{:S(2)}) %collective-permute-start.3) | collective-permute-done | bytes 262176 | tf_op jit(solution)/shard_map/ppermute | solution.py:292
  106.7 3.1 %collective-permute-done.4.refs_2_ = bf16[32,16,256]{2,1,0:T(8,128)(2,1)S(1)} collective-permute-done((bf16[32,16,256]{2,1,0:T(8,128)(2,1)S(1)}, bf16[32,16,256]{2,1,0:T(8,128)(2,1)S(1)}, u32[]{:S(2)}, u32[]{:S(2)}) %collective-permute-start.4) | collective-permute-done | bytes 262176 | tf_op jit(solution)/shard_map/ppermute | solution.py:292
  109.9 2.3 %collective-permute-done.5.refs_3_ = bf16[32,16,256]{2,1,0:T(8,128)(2,1)S(1)} collective-permute-done((bf16[32,16,256]{2,1,0:T(8,128)(2,1)S(1)}, bf16[32,16,256]{2,1,0:T(8,128)(2,1)S(1)}, u32[]{:S(2)}, u32[]{:S(2)}) %collective-permute-start.5) | collective-permute-done | bytes 262176 | tf_op jit(solution)/shard_map/ppermute | solution.py:292
  112.2 0.1 add.7
  112.3 2.0 %collective-permute-start.6 = (bf16[8,16,256]{2,1,0:T(8,128)(2,1)S(1)}, bf16[8,16,256]{2,1,0:T(8,128)(2,1)S(1)}, u32[]{:S(2)}, u32[]{:S(2)}) collective-permute-start(bf16[8,16,256]{2,1,0:T(8,128)(2,1)S(1)} %get-tuple-element.36), channel_id=1, source_target_pairs={{0,16},{1,65},{2,18},{3,67},{4,20},{5,69},{6,22},{7,71},{8,24},{9,... | collective-permute-start | bytes 196616 | tf_op jit(solution)/shard_map/ppermute | solution.py:292
  114.3 2.9 %collective-permute-start.7 = (bf16[8,16,256]{2,1,0:T(8,128)(2,1)S(1)}, bf16[8,16,256]{2,1,0:T(8,128)(2,1)S(1)}, u32[]{:S(2)}, u32[]{:S(2)}) collective-permute-start(bf16[8,16,256]{2,1,0:T(8,128)(2,1)S(1)} %get-tuple-element.37), channel_id=1, source_target_pairs={{0,32},{1,129},{2,34},{3,131},{4,36},{5,133},{6,38},{7,135},{8,40}... | collective-permute-start | bytes 196616 | tf_op jit(solution)/shard_map/ppermute | solution.py:292
  117.2 0.7 collective-permute-start.8
  117.9 0.1 collective-permute-done.6.refs_1_
  118.0 2.2 %collective-permute-done.7.refs_2_ = bf16[8,16,256]{2,1,0:T(8,128)(2,1)S(1)} collective-permute-done((bf16[8,16,256]{2,1,0:T(8,128)(2,1)S(1)}, bf16[8,16,256]{2,1,0:T(8,128)(2,1)S(1)}, u32[]{:S(2)}, u32[]{:S(2)}) %collective-permute-start.7) | collective-permute-done | bytes 65568 | tf_op jit(solution)/shard_map/ppermute | solution.py:292
  120.2 1.3 collective-permute-done.8.refs_3_
  121.5 1.6 %collective-permute-start.9 = (bf16[4,16,256]{2,1,0:T(8,128)(2,1)S(1)}, bf16[4,16,256]{2,1,0:T(8,128)(2,1)S(1)}, u32[]{:S(2)}, u32[]{:S(2)}) collective-permute-start(bf16[4,16,256]{2,1,0:T(8,128)(2,1)S(1)} %get-tuple-element.40), channel_id=1, source_target_pairs={{0,14},{1,15},{2,12},{3,13},{4,10},{5,11},{6,8},{7,9},{8,6},{9,7},... | collective-permute-start | bytes 98312 | tf_op jit(solution)/shard_map/ppermute | solution.py:292
  123.1 4.0 %collective-permute-done.9.refs_1_ = bf16[4,16,256]{2,1,0:T(8,128)(2,1)S(1)} collective-permute-done((bf16[4,16,256]{2,1,0:T(8,128)(2,1)S(1)}, bf16[4,16,256]{2,1,0:T(8,128)(2,1)S(1)}, u32[]{:S(2)}, u32[]{:S(2)}) %collective-permute-start.9) | collective-permute-done | bytes 32800 | tf_op jit(solution)/shard_map/ppermute | solution.py:292
  127.1 2.0 %collective-permute-start.10 = (bf16[2,16,256]{2,1,0:T(8,128)(2,1)S(1)}, bf16[2,16,256]{2,1,0:T(8,128)(2,1)S(1)}, u32[]{:S(2)}, u32[]{:S(2)}) collective-permute-start(bf16[2,16,256]{2,1,0:T(8,128)(2,1)S(1)} %get-tuple-element.42), channel_id=1, source_target_pairs={{0,4},{1,5},{2,6},{3,7},{4,0},{5,1},{6,2},{7,3},{8,12},{9,13},{10,... | collective-permute-start | bytes 49160 | tf_op jit(solution)/shard_map/ppermute | solution.py:292
  129.2 2.7 %collective-permute-done.10.refs_1_ = bf16[2,16,256]{2,1,0:T(8,128)(2,1)S(1)} collective-permute-done((bf16[2,16,256]{2,1,0:T(8,128)(2,1)S(1)}, bf16[2,16,256]{2,1,0:T(8,128)(2,1)S(1)}, u32[]{:S(2)}, u32[]{:S(2)}) %collective-permute-start.10) | collective-permute-done | bytes 16416 | tf_op jit(solution)/shard_map/ppermute | solution.py:292
  131.8 1.3 collective-permute-start.11
  133.1 2.4 %collective-permute-done.11.refs_1_ = bf16[1,16,256]{2,1,0:T(8,128)(2,1)S(1)} collective-permute-done((bf16[1,16,256]{2,1,0:T(8,128)(2,1)S(1)}, bf16[1,16,256]{2,1,0:T(8,128)(2,1)S(1)}, u32[]{:S(2)}, u32[]{:S(2)}) %collective-permute-start.11) | collective-permute-done | bytes 8224 | tf_op jit(solution)/shard_map/ppermute | solution.py:292
  135.5 0.6 add.11
  (11 shorter events, 0.1 us)
Async XLA Ops:
  4.3 28.3 %all-to-all-start = ((bf16[32,16,480]{2,1,0:T(8,128)(2,1)}), bf16[32,16,480]{2,1,0:T(8,128)(2,1)S(1)}, u32[]{:S(2)}, u32[]{:S(2)}) async-start(bf16[32,16,480]{2,1,0:T(8,128)(2,1)} %get-tuple-element.26), calls=%async_computation | async-start | bytes 1048576 | tf_op jit(solution)/shard_map/all_to_all | solution.py:358
  14.1 10.8 %collective-permute-start = (bf16[32,16,256]{2,1,0:T(8,128)(2,1)}, bf16[32,16,256]{2,1,0:T(8,128)(2,1)S(1)}, u32[]{:S(2)}, u32[]{:S(2)}) collective-permute-start(bf16[32,16,256]{2,1,0:T(8,128)(2,1)} %get-tuple-element.24.tail_ref), channel_id=1, source_target_pairs={{0,1},{1,2},{2,3},{3,4},{4,5},{5,6},{6,7},{7,8},{8,9},{9,10},{10,1... | collective-permute-start | bytes 786440 | tf_op jit(solution)/shard_map/ppermute | solution.py:355
  16.3 8.6 %collective-permute-start.1 = (bf16[32,16,256]{2,1,0:T(8,128)(2,1)}, bf16[32,16,256]{2,1,0:T(8,128)(2,1)S(1)}, u32[]{:S(2)}, u32[]{:S(2)}) collective-permute-start(bf16[32,16,256]{2,1,0:T(8,128)(2,1)} %get-tuple-element.25.head_ref), channel_id=1, source_target_pairs={{1,0},{2,1},{3,2},{4,3},{5,4},{6,5},{7,6},{8,7},{9,8},{10,9},{11,1... | collective-permute-start | bytes 786440 | tf_op jit(solution)/shard_map/ppermute | solution.py:356
  25.0 7.6 %copy-start.2 = (bf16[32,16,256]{2,1,0:T(8,128)(2,1)}, bf16[32,16,256]{2,1,0:T(8,128)(2,1)S(1)}, u32[]{:S(2)}) copy-start(bf16[32,16,256]{2,1,0:T(8,128)(2,1)S(1)} %collective-permute-done.before_ref) | copy-start | bytes 786436
  25.0 7.6 %copy-start.3 = (bf16[32,16,256]{2,1,0:T(8,128)(2,1)}, bf16[32,16,256]{2,1,0:T(8,128)(2,1)S(1)}, u32[]{:S(2)}) copy-start(bf16[32,16,256]{2,1,0:T(8,128)(2,1)S(1)} %collective-permute-done.1.after_ref) | copy-start | bytes 786436
  32.6 0.8 copy-start.1
  95.7 3.0 %collective-permute-start.2 = (bf16[128,16,256]{2,1,0:T(8,128)(2,1)}, bf16[128,16,256]{2,1,0:T(8,128)(2,1)S(1)}, u32[]{:S(2)}, u32[]{:S(2)}) collective-permute-start(bf16[128,16,256]{2,1,0:T(8,128)(2,1)} %bitcast.5), channel_id=1, source_target_pairs={{0,1},{1,0},{2,3},{3,2},{4,5},{5,4},{6,7},{7,6},{8,9},{9,8},{10,11... | collective-permute-start | bytes 3145736 | tf_op jit(solution)/shard_map/ppermute | solution.py:292
  98.7 1.2 copy-start
  100.3 6.4 %collective-permute-start.3 = (bf16[32,16,256]{2,1,0:T(8,128)(2,1)S(1)}, bf16[32,16,256]{2,1,0:T(8,128)(2,1)S(1)}, u32[]{:S(2)}, u32[]{:S(2)}) collective-permute-start(bf16[32,16,256]{2,1,0:T(8,128)(2,1)S(1)} %get-tuple-element.32), channel_id=1, source_target_pairs={{0,64},{1,17},{2,66},{3,19},{4,68},{5,21},{6,70},{7,23},{8,72},{9,... | collective-permute-start | bytes 786440 | tf_op jit(solution)/shard_map/ppermute | solution.py:292
  101.9 8.0 %collective-permute-start.4 = (bf16[32,16,256]{2,1,0:T(8,128)(2,1)S(1)}, bf16[32,16,256]{2,1,0:T(8,128)(2,1)S(1)}, u32[]{:S(2)}, u32[]{:S(2)}) collective-permute-start(bf16[32,16,256]{2,1,0:T(8,128)(2,1)S(1)} %get-tuple-element.33), channel_id=1, source_target_pairs={{0,128},{1,33},{2,130},{3,35},{4,132},{5,37},{6,134},{7,39},{8,136... | collective-permute-start | bytes 786440 | tf_op jit(solution)/shard_map/ppermute | solution.py:292
  103.0 9.2 %collective-permute-start.5 = (bf16[32,16,256]{2,1,0:T(8,128)(2,1)S(1)}, bf16[32,16,256]{2,1,0:T(8,128)(2,1)S(1)}, u32[]{:S(2)}, u32[]{:S(2)}) collective-permute-start(bf16[32,16,256]{2,1,0:T(8,128)(2,1)S(1)} %get-tuple-element.34), channel_id=1, source_target_pairs={{0,192},{1,49},{2,194},{3,51},{4,196},{5,53},{6,198},{7,55},{8,200... | collective-permute-start | bytes 786440 | tf_op jit(solution)/shard_map/ppermute | solution.py:292
  112.3 5.7 %collective-permute-start.6 = (bf16[8,16,256]{2,1,0:T(8,128)(2,1)S(1)}, bf16[8,16,256]{2,1,0:T(8,128)(2,1)S(1)}, u32[]{:S(2)}, u32[]{:S(2)}) collective-permute-start(bf16[8,16,256]{2,1,0:T(8,128)(2,1)S(1)} %get-tuple-element.36), channel_id=1, source_target_pairs={{0,16},{1,65},{2,18},{3,67},{4,20},{5,69},{6,22},{7,71},{8,24},{9,... | collective-permute-start | bytes 196616 | tf_op jit(solution)/shard_map/ppermute | solution.py:292
  114.3 5.8 %collective-permute-start.7 = (bf16[8,16,256]{2,1,0:T(8,128)(2,1)S(1)}, bf16[8,16,256]{2,1,0:T(8,128)(2,1)S(1)}, u32[]{:S(2)}, u32[]{:S(2)}) collective-permute-start(bf16[8,16,256]{2,1,0:T(8,128)(2,1)S(1)} %get-tuple-element.37), channel_id=1, source_target_pairs={{0,32},{1,129},{2,34},{3,131},{4,36},{5,133},{6,38},{7,135},{8,40}... | collective-permute-start | bytes 196616 | tf_op jit(solution)/shard_map/ppermute | solution.py:292
  117.2 4.3 %collective-permute-start.8 = (bf16[8,16,256]{2,1,0:T(8,128)(2,1)S(1)}, bf16[8,16,256]{2,1,0:T(8,128)(2,1)S(1)}, u32[]{:S(2)}, u32[]{:S(2)}) collective-permute-start(bf16[8,16,256]{2,1,0:T(8,128)(2,1)S(1)} %get-tuple-element.38), channel_id=1, source_target_pairs={{0,48},{1,193},{2,50},{3,195},{4,52},{5,197},{6,54},{7,199},{8,56}... | collective-permute-start | bytes 196616 | tf_op jit(solution)/shard_map/ppermute | solution.py:292
  121.5 5.6 %collective-permute-start.9 = (bf16[4,16,256]{2,1,0:T(8,128)(2,1)S(1)}, bf16[4,16,256]{2,1,0:T(8,128)(2,1)S(1)}, u32[]{:S(2)}, u32[]{:S(2)}) collective-permute-start(bf16[4,16,256]{2,1,0:T(8,128)(2,1)S(1)} %get-tuple-element.40), channel_id=1, source_target_pairs={{0,14},{1,15},{2,12},{3,13},{4,10},{5,11},{6,8},{7,9},{8,6},{9,7},... | collective-permute-start | bytes 98312 | tf_op jit(solution)/shard_map/ppermute | solution.py:292
  127.1 4.7 %collective-permute-start.10 = (bf16[2,16,256]{2,1,0:T(8,128)(2,1)S(1)}, bf16[2,16,256]{2,1,0:T(8,128)(2,1)S(1)}, u32[]{:S(2)}, u32[]{:S(2)}) collective-permute-start(bf16[2,16,256]{2,1,0:T(8,128)(2,1)S(1)} %get-tuple-element.42), channel_id=1, source_target_pairs={{0,4},{1,5},{2,6},{3,7},{4,0},{5,1},{6,2},{7,3},{8,12},{9,13},{10,... | collective-permute-start | bytes 49160 | tf_op jit(solution)/shard_map/ppermute | solution.py:292
  131.8 3.7 %collective-permute-start.11 = (bf16[1,16,256]{2,1,0:T(8,128)(2,1)S(1)}, bf16[1,16,256]{2,1,0:T(8,128)(2,1)S(1)}, u32[]{:S(2)}, u32[]{:S(2)}) collective-permute-start(bf16[1,16,256]{2,1,0:T(8,128)(2,1)S(1)} %get-tuple-element.44), channel_id=1, source_target_pairs={{0,2},{1,3},{2,0},{3,1},{4,6},{5,7},{6,4},{7,5},{8,10},{9,11},{10,... | collective-permute-start | bytes 24584 | tf_op jit(solution)/shard_map/ppermute | solution.py:292

commit v2 on v1

--- a/solution.py
+++ b/solution.py
@@ -68,9 +68,9 @@
     return pl.pallas_call(
         lift_kernel,
         out_shape=[edge, edge, shape],
-        grid=(4,),
-        in_specs=[pl.BlockSpec((half // 2, CHANNELS, TILE), lambda i: (i, 0, 0))],
-        out_specs=[pl.BlockSpec((half // 4, CHANNELS, n), lambda i: (i, 0, 0)) for n in (ROW, ROW, TILE)],
+        grid=(2,),
+        in_specs=[pl.BlockSpec((half, CHANNELS, TILE), lambda i: (i, 0, 0))],
+        out_specs=[pl.BlockSpec((half // 2, CHANNELS, n), lambda i: (i, 0, 0)) for n in (ROW, ROW, TILE)],
         name="lift",
         compiler_params=pltpu.CompilerParams(vmem_limit_bytes=60 * MIB),
     )(latents)
@@ -122,29 +122,32 @@
     return copies
 
 
-def slotted(values, codes_line):
-    slot = codes_line >> 14
-    blank = jnp.zeros((16, LINE), f32)
-    pieces = []
-    for s in range(4):
-        pieces += [blank, jnp.where(slot == s, values, 0.0)]
-    return jnp.concatenate(pieces, axis=0).astype(bf16)
-
-
-def place_pair(first, second, eye, vals_ref, u):
+def slotted(values, slot):
+    return [jnp.where(slot == s, values, 0.0) for s in range(4)]
+
+
+def spaced(pieces):
+    blank = jnp.zeros((16, LINE), bf16)
+    return jnp.concatenate([v for p in pieces for v in (blank, p.astype(bf16))], axis=0)
+
+
+def vals_rows(group, k, start, count):
+    return pl.ds((group * LINE + start) * 8 + k, count, stride=8)
+
+
+def place_pair(first, second, same, eye, vals_ref, group, k):
+    second = [b + jnp.where(same, a, 0.0) for a, b in zip(first, second)]
+    first, second = spaced(first), spaced(second)
     for h in range(2):
         at = slice(256 * h, 256 * h + 256)
         block = nt(eye, jnp.concatenate([first[:, at], second[:, at]], axis=0))
-        for k in range(2):
-            start = pl.multiple_of((u + k) * LINE + 256 * h, 256)
-            vals_ref[pl.ds(start, 256), :] = block[:, 128 * k : 128 * k + 128]
-
-
-def looked_up(vals_ref, codes_line, pick, u):
-    start = pl.multiple_of(u * LINE, LINE)
-    rows = vals_ref[pl.ds(start, LINE), :].astype(bf16)
+        vals_ref[vals_rows(group, k, 256 * h, 256), :] = block[:, :128]
+        vals_ref[vals_rows(group, k + 4, 256 * h, 256), :] = block[:, 128:]
+
+
+def looked_up(vals_ref, slot, pick, group, k):
+    rows = vals_ref[vals_rows(group, k, 0, LINE), :].astype(bf16)
     parts = nt(pick, rows)
-    slot = codes_line >> 14
     out = parts[:16]
     for s in range(1, 4):
         out = jnp.where(slot == s, parts[s * 16 : (s + 1) * 16], out)
@@ -152,17 +155,27 @@
 
 
 def walk(smem, vals_ref, tables, start, stop):
-    def step(g, carry):
-        for base in range(0, LINES, TABLES):
-            at = [smem[base + t][g] for t in range(TABLES)]
-            rows = [tables[t][pl.ds(at[t], 1), :] for t in range(TABLES)]
-            adds = [vals_ref[pl.ds((base + t) * LINE + g, 1), :] for t in range(TABLES)]
-            for t in range(TABLES):
-                vals_ref[pl.ds((base + t) * LINE + g, 1), :] = rows[t]
-                tables[t][pl.ds(at[t], 1), :] = rows[t] + adds[t]
-        return carry
-
-    lax.fori_loop(start, stop, step, 0)
+    sub = lax.broadcasted_iota(jnp.int32, (8, 128), 0)
+
+    def one(g):
+        for group in range(LINES // 8):
+            here = pl.ds(pl.multiple_of((group * LINE + g) * 8, 8), 8)
+            tile = vals_ref[here, :]
+            at = [pl.ds(smem[group * 8 + k][g] + (8 - k), 8) for k in range(8)]
+            rows = [tables[k % TABLES][at[k], :] for k in range(8)]
+            for k in range(8):
+                pltpu.store(tables[k % TABLES].at[at[k], :], rows[k] + tile, mask=sub == k)
+            out = rows[0]
+            for k in range(1, 8):
+                out = jnp.where(sub == k, rows[k], out)
+            vals_ref[here, :] = out
+
+    def step(i, carry):
+        one(start + 2 * i)
+        one(start + 2 * i + 1)
+        return carry
+
+    lax.fori_loop(0, (stop - start) // 2, step, 0)
 
 
 def quantize_kernel(before_ref, head_ref, tail_ref, after_ref, values_ref, weights_ref, fine_codes_ref, coarse_codes_ref,
@@ -170,7 +183,7 @@
                     t0, t1, t2, t3, vals_ref, enc_ref, fine_padded, coarse_padded, fine_rows, coarse_rows, *rest):
     fine_smem, coarse_smem, (fine_sem, coarse_sem, in_sem) = rest[:LINES], rest[LINES : 2 * LINES], rest[2 * LINES :]
     tables = [t0, t1, t2, t3]
-    fetch = pltpu.make_async_copy(table_in, t0, in_sem)
+    fetch = pltpu.make_async_copy(table_in, t0.at[pl.ds(8, ROWS), :], in_sem)
     fetch.start()
     gap = jnp.zeros((LINES, ROW - WIDTH), jnp.int32)
     fine_padded[...] = jnp.concatenate([fine_codes_ref[:, :WIDTH], gap, fine_codes_ref[:, WIDTH:], gap], axis=1)
@@ -191,19 +204,20 @@
         stacked = jnp.concatenate(pieces, axis=0)
         enc = jnp.concatenate([lines[1], lines[2]], axis=1) + jnp.dot(weights, stacked, preferred_element_type=f32)
         enc_ref[u] = enc
-        return slotted(enc, fine_padded[pl.ds(u, 1), :])
-
-    def encode(p, carry):
-        for k in range(2):
-            u = 4 * p + 2 * k
-            place_pair(encoded(u), encoded(u + 1), eye, vals_ref, u)
-        return carry
-
-    lax.fori_loop(0, LINES // 4, encode, 0)
+        return slotted(enc, fine_padded[pl.ds(u, 1), :] >> 14)
+
+    def encode(group, carry):
+        for k in range(4):
+            u = 8 * group + k
+            same = fine_rows[pl.ds(u, 1), :] == fine_rows[pl.ds(u + 4, 1), :]
+            place_pair(encoded(u), encoded(u + 4), same, eye, vals_ref, group, k)
+        return carry
+
+    lax.fori_loop(0, LINES // 8, encode, 0)
     fetch.wait()
 
     def spread(i, carry):
-        at = pl.ds(pl.multiple_of(i * 64, 64), 64)
+        at = pl.ds(pl.multiple_of(i * 64 + 8, 8), 64)
         code_part = t0[at, :]
         for t in tables[1:]:
             t[at, :] = code_part
@@ -219,19 +233,20 @@
 
     def slots_of(u):
         values = jnp.concatenate([values_ref[u].astype(f32), tail_gap], axis=1)
-        return slotted(values, coarse_padded[pl.ds(u, 1), :])
-
-    def turn(p, carry):
+        return slotted(values, coarse_padded[pl.ds(u, 1), :] >> 14)
+
+    def turn(group, carry):
+        for k in range(8):
+            u = 8 * group + k
+            error = enc_ref[u] - looked_up(vals_ref, fine_padded[pl.ds(u, 1), :] >> 14, pick, group, k)
+            fine_error_ref[u] = jnp.concatenate([error[:, :WIDTH], error[:, ROW : ROW + WIDTH]], axis=1).astype(bf16)
         for k in range(4):
-            u = 4 * p + k
-            error = enc_ref[u] - looked_up(vals_ref, fine_padded[pl.ds(u, 1), :], pick, u)
-            fine_error_ref[u] = jnp.concatenate([error[:, :WIDTH], error[:, ROW : ROW + WIDTH]], axis=1).astype(bf16)
-        for k in range(2):
-            u = 4 * p + 2 * k
-            place_pair(slots_of(u), slots_of(u + 1), eye, vals_ref, u)
-        return carry
-
-    lax.fori_loop(0, LINES // 4, turn, 0)
+            u = 8 * group + k
+            same = coarse_rows[pl.ds(u, 1), :] == coarse_rows[pl.ds(u + 4, 1), :]
+            place_pair(slots_of(u), slots_of(u + 4), same, eye, vals_ref, group, k)
+        return carry
+
+    lax.fori_loop(0, LINES // 8, turn, 0)
     for c in coarse_copies:
         c.wait()
     walk(coarse_smem, vals_ref, tables, 0, TILE)
@@ -240,7 +255,7 @@
     def total(i, carry):
         for out_ref, core in ((send_ref, 1 - my_core), (keep_ref, my_core)):
             b = 2 * i + core
-            at = pl.ds(pl.multiple_of(b * 256, 256), 256)
+            at = pl.ds(pl.multiple_of(b * 256 + 8, 8), 256)
             summed = t0[at, :] + t1[at, :] + t2[at, :] + t3[at, :]
             parts = nt(pick_sum, summed.astype(bf16)).astype(bf16)
             y_off = ((b >> 4) - my_y) & 3
@@ -258,7 +273,7 @@
         parts = []
         for k in range(4):
             u = 4 * q + k
-            looked = looked_up(vals_ref, coarse_padded[u : u + 1, :], pick, u)
+            looked = looked_up(vals_ref, coarse_padded[u : u + 1, :] >> 14, pick, u // 8, u % 8)
             parts.append(values_ref[u].astype(f32) - looked[:, :TILE])
         coarse_error_ref[0, :, q * 4 * TILE : (q + 1) * 4 * TILE] = jnp.concatenate(parts, axis=1).astype(bf16)
 
@@ -271,13 +286,13 @@
                    jax.ShapeDtypeStruct((1, CHANNELS, LINES * TILE), bf16), sums, sums],
         in_specs=[VMEM] * 11 + [HBM],
         out_specs=[VMEM] * 4,
-        scratch_shapes=[pltpu.VMEM((ROWS, 128), f32)] * TABLES
+        scratch_shapes=[pltpu.VMEM((ROWS + 16, 128), f32)] * TABLES
         + [pltpu.VMEM((LINES * LINE, 128), f32), pltpu.VMEM((LINES, CHANNELS, LINE), f32)]
         + [pltpu.VMEM((LINES, LINE), jnp.int32)] * 4
         + [pltpu.SMEM((LINE,), jnp.int32)] * (2 * LINES)
         + [pltpu.SemaphoreType.DMA((LINES,)), pltpu.SemaphoreType.DMA((LINES,)), pltpu.SemaphoreType.DMA],
         name="quantize",
-        compiler_params=pltpu.CompilerParams(vmem_limit_bytes=58 * MIB),
+        compiler_params=pltpu.CompilerParams(vmem_limit_bytes=50 * MIB),
         cost_estimate=pl.CostEstimate(flops=10**9, bytes_accessed=10**8, transcendentals=0),
     )(before, head, tail, after, values, weights, fine_codes, coarse_codes, identity(), pick_matrix(0), pick_matrix(16), table)
 

time: 136 us -> 124 us (0.912)
  Pallas kernels: 74.5 us -> 64.3 us
  waiting for transfers between devices: 30.1 us -> 27.5 us
  local copies, waits for them, and re-layouts: 2.04 us -> 0.04 us
  starting transfers between devices: 28.8 us -> 30.4 us
    pallas_call x1, Pallas kernels: 62.3 us -> 53.2 us  [quantize(): pl.pallas_call(quantize_kernel, out_shape=[jax.ShapeDtypeStruct((LINES, C...]
    ppermute x10, waiting for transfers between devices: 22.5 us -> 19.9 us  [permuted(): return lax.ppermute(value, CORES, pairs)]
    unnamed x8 -> x16, local copies, waits for them, and re-layouts: 2.04 us -> 0.04 us
    ppermute x10, starting transfers between devices: 15.4 us -> 16.9 us  [permuted(): return lax.ppermute(value, CORES, pairs)]
  transfers between devices with their start and end apart: 13 -> 13, of which waited for: 11 -> 10; matrix products, arithmetic and copies ran while one was open for 0% -> 0% of each run, Pallas kernels for 5% -> 6%
where the time goes in v2:
time: 124 us; the launch traced here: 123 us
  Pallas kernels  64.3 us (52%)
  starting transfers between devices  30.4 us (25%)
  waiting for transfers between devices  27.5 us (22%)
    pallas_call x1, Pallas kernels, quantize(): pl.pallas_call(quantize_kernel, out_shape=[jax.ShapeDtypeStruct((LINES, C...  53.2 us
    ppermute x10, waiting for transfers between devices, permuted(): return lax.ppermute(value, CORES, pairs)  19.9 us
    ppermute x10, starting transfers between devices, permuted(): return lax.ppermute(value, CORES, pairs)  16.9 us
    all_to_all x1, starting transfers between devices, shards(): lax.all_to_all(lifted, SPACE, split_axis=0, concat_axis=0, tiled=True)  10 us
    all_to_all x1, waiting for transfers between devices, shards(): lax.all_to_all(lifted, SPACE, split_axis=0, concat_axis=0, tiled=True)  7.55 us
    pallas_call x1, Pallas kernels, code_table(): pl.pallas_call(table_kernel, grid=(ROWS // 2048,), out_shape=jax.ShapeDty...  7.39 us
    pallas_call x1, Pallas kernels, lift(): pl.pallas_call(lift_kernel, out_shape=[edge, edge, shape], grid=(2,), in_...  2.48 us
  transfers between devices with their start and end apart: 13, of which 10 were waited for; matrix products, arithmetic and copies ran while one was open for 0% of the time, Pallas kernels for 6%

profile of v2, /device:TPU:2, one launch (start us, length us, event | category | flops | bytes accessed | tf_op | source)
XLA Modules:
  0.0 123.0 jit_solution(6143416698934391111)
XLA Ops:
  0.6 0.0 copy-start
  0.6 0.0 copy-start.5
  0.7 0.0 copy-start.6
  0.7 2.5 %lift.1 = (bf16[32,16,256]{2,1,0:T(8,128)(2,1)}, bf16[32,16,256]{2,1,0:T(8,128)(2,1)}, bf16[32,16,480]{2,1,0:T(8,128)(2,1)}) custom-call(bf16[64,16,480]{2,1,0:T(8,128)(2,1)} %lat_ref.1), custom_call_target="tpu_custom_call" | custom-call | tf_op jit(solution)/shard_map/lift/pallas_call | solution.py:68
  3.2 10.0 %all-to-all-start = ((bf16[32,16,480]{2,1,0:T(8,128)(2,1)}), bf16[32,16,480]{2,1,0:T(8,128)(2,1)S(1)}, u32[]{:S(2)}, u32[]{:S(2)}) async-start(bf16[32,16,480]{2,1,0:T(8,128)(2,1)} %get-tuple-element.26), calls=%async_computation | async-start | bytes 1048576 | tf_op jit(solution)/shard_map/all_to_all | solution.py:373
  13.2 2.2 %collective-permute-start = (bf16[32,16,256]{2,1,0:T(8,128)(2,1)}, bf16[32,16,256]{2,1,0:T(8,128)(2,1)S(1)}, u32[]{:S(2)}, u32[]{:S(2)}) collective-permute-start(bf16[32,16,256]{2,1,0:T(8,128)(2,1)} %get-tuple-element.24.tail_ref), channel_id=1, source_target_pairs={{0,1},{1,2},{2,3},{3,4},{4,5},{5,6},{6,7},{7,8},{8,9},{9,10},{10,1... | collective-permute-start | bytes 786440 | tf_op jit(solution)/shard_map/ppermute | solution.py:370
  15.4 1.3 %collective-permute-start.1 = (bf16[32,16,256]{2,1,0:T(8,128)(2,1)}, bf16[32,16,256]{2,1,0:T(8,128)(2,1)S(1)}, u32[]{:S(2)}, u32[]{:S(2)}) collective-permute-start(bf16[32,16,256]{2,1,0:T(8,128)(2,1)} %get-tuple-element.25.head_ref), channel_id=1, source_target_pairs={{1,0},{2,1},{3,2},{4,3},{5,4},{6,5},{7,6},{8,7},{9,8},{10,9},{11,1... | collective-permute-start | bytes 786440 | tf_op jit(solution)/shard_map/ppermute | solution.py:371
  16.7 7.4 %code_table.1.table_in = f32[16384,128]{1,0:T(8,128)} custom-call(bf16[16,65536]{1,0:T(8,128)(2,1)} %codebook_ref.1, bf16[256,256]{1,0:T(8,128)(2,1)} %constant.6.clone.eye_ref), custom_call_target="tpu_custom_call" | custom-call | flops 1000000000 | bytes 10000000 | tf_op jit(solution)/shard_map/code_table/pallas_call | solution.py:97
  24.1 7.5 %all-to-all-done.values_ref = bf16[32,16,480]{2,1,0:T(8,128)(2,1)S(1)} async-done(((bf16[32,16,480]{2,1,0:T(8,128)(2,1)}), bf16[32,16,480]{2,1,0:T(8,128)(2,1)S(1)}, u32[]{:S(2)}, u32[]{:S(2)}) %all-to-all-start) | async-done | bytes 491552 | tf_op jit(solution)/shard_map/all_to_all | solution.py:373
  31.7 53.2 %quantize.1 = (bf16[32,16,480]{2,1,0:T(8,128)(2,1)}, bf16[1,16,15360]{2,1,0:T(8,128)(2,1)}, bf16[4,4,8,16,256]{4,3,2,1,0:T(8,128)(2,1)S(1)}, bf16[4,4,8,16,256]{4,3,2,1,0:T(8,128)(2,1)S(1)}) custom-call(bf16[32,16,256]{2,1,0:T(8,128)(2,1)S(1)} %collective-permute-done.before_ref, bf16[32,16,256]{2,1,0:T(8,128)(2,1)S(1)} %copy-done.1, ...), custom_call_target="tpu_custom_call" | custom-call | flops 1000000000 | bytes 100000000 | tf_op jit(solution)/shard_map/quantize/pallas_call | solution.py:283
  85.0 0.1 collective-permute-start.2
  85.1 2.6 %collective-permute-done.2.refs_1_ = bf16[128,16,256]{2,1,0:T(8,128)(2,1)S(1)} collective-permute-done((bf16[128,16,256]{2,1,0:T(8,128)(2,1)S(1)}, bf16[128,16,256]{2,1,0:T(8,128)(2,1)S(1)}, u32[]{:S(2)}, u32[]{:S(2)}) %collective-permute-start.2) | collective-permute-done | bytes 1048608 | tf_op jit(solution)/shard_map/ppermute | solution.py:307
  87.7 0.4 add.6
  88.1 1.6 %collective-permute-start.3 = (bf16[32,16,256]{2,1,0:T(8,128)(2,1)S(1)}, bf16[32,16,256]{2,1,0:T(8,128)(2,1)S(1)}, u32[]{:S(2)}, u32[]{:S(2)}) collective-permute-start(bf16[32,16,256]{2,1,0:T(8,128)(2,1)S(1)} %get-tuple-element.32), channel_id=1, source_target_pairs={{0,64},{1,17},{2,66},{3,19},{4,68},{5,21},{6,70},{7,23},{8,72},{9,... | collective-permute-start | bytes 786440 | tf_op jit(solution)/shard_map/ppermute | solution.py:307
  89.7 1.1 collective-permute-start.4
  90.8 2.2 %collective-permute-start.5 = (bf16[32,16,256]{2,1,0:T(8,128)(2,1)S(1)}, bf16[32,16,256]{2,1,0:T(8,128)(2,1)S(1)}, u32[]{:S(2)}, u32[]{:S(2)}) collective-permute-start(bf16[32,16,256]{2,1,0:T(8,128)(2,1)S(1)} %get-tuple-element.34), channel_id=1, source_target_pairs={{0,192},{1,49},{2,194},{3,51},{4,196},{5,53},{6,198},{7,55},{8,200... | collective-permute-start | bytes 786440 | tf_op jit(solution)/shard_map/ppermute | solution.py:307
  92.9 1.6 %collective-permute-done.3.refs_1_ = bf16[32,16,256]{2,1,0:T(8,128)(2,1)S(1)} collective-permute-done((bf16[32,16,256]{2,1,0:T(8,128)(2,1)S(1)}, bf16[32,16,256]{2,1,0:T(8,128)(2,1)S(1)}, u32[]{:S(2)}, u32[]{:S(2)}) %collective-permute-start.3) | collective-permute-done | bytes 262176 | tf_op jit(solution)/shard_map/ppermute | solution.py:307
  94.5 3.1 %collective-permute-done.4.refs_2_ = bf16[32,16,256]{2,1,0:T(8,128)(2,1)S(1)} collective-permute-done((bf16[32,16,256]{2,1,0:T(8,128)(2,1)S(1)}, bf16[32,16,256]{2,1,0:T(8,128)(2,1)S(1)}, u32[]{:S(2)}, u32[]{:S(2)}) %collective-permute-start.4) | collective-permute-done | bytes 262176 | tf_op jit(solution)/shard_map/ppermute | solution.py:307
  97.6 2.3 %collective-permute-done.5.refs_3_ = bf16[32,16,256]{2,1,0:T(8,128)(2,1)S(1)} collective-permute-done((bf16[32,16,256]{2,1,0:T(8,128)(2,1)S(1)}, bf16[32,16,256]{2,1,0:T(8,128)(2,1)S(1)}, u32[]{:S(2)}, u32[]{:S(2)}) %collective-permute-start.5) | collective-permute-done | bytes 262176 | tf_op jit(solution)/shard_map/ppermute | solution.py:307
  99.9 0.1 add.7
  100.1 1.3 %collective-permute-start.6 = (bf16[8,16,256]{2,1,0:T(8,128)(2,1)S(1)}, bf16[8,16,256]{2,1,0:T(8,128)(2,1)S(1)}, u32[]{:S(2)}, u32[]{:S(2)}) collective-permute-start(bf16[8,16,256]{2,1,0:T(8,128)(2,1)S(1)} %get-tuple-element.36), channel_id=1, source_target_pairs={{0,16},{1,65},{2,18},{3,67},{4,20},{5,69},{6,22},{7,71},{8,24},{9,... | collective-permute-start | bytes 196616 | tf_op jit(solution)/shard_map/ppermute | solution.py:307
  101.4 2.9 %collective-permute-start.7 = (bf16[8,16,256]{2,1,0:T(8,128)(2,1)S(1)}, bf16[8,16,256]{2,1,0:T(8,128)(2,1)S(1)}, u32[]{:S(2)}, u32[]{:S(2)}) collective-permute-start(bf16[8,16,256]{2,1,0:T(8,128)(2,1)S(1)} %get-tuple-element.37), channel_id=1, source_target_pairs={{0,32},{1,129},{2,34},{3,131},{4,36},{5,133},{6,38},{7,135},{8,40}... | collective-permute-start | bytes 196616 | tf_op jit(solution)/shard_map/ppermute | solution.py:307
  104.3 1.4 %collective-permute-start.8 = (bf16[8,16,256]{2,1,0:T(8,128)(2,1)S(1)}, bf16[8,16,256]{2,1,0:T(8,128)(2,1)S(1)}, u32[]{:S(2)}, u32[]{:S(2)}) collective-permute-start(bf16[8,16,256]{2,1,0:T(8,128)(2,1)S(1)} %get-tuple-element.38), channel_id=1, source_target_pairs={{0,48},{1,193},{2,50},{3,195},{4,52},{5,197},{6,54},{7,199},{8,56}... | collective-permute-start | bytes 196616 | tf_op jit(solution)/shard_map/ppermute | solution.py:307
  105.7 1.5 %collective-permute-done.7.refs_2_ = bf16[8,16,256]{2,1,0:T(8,128)(2,1)S(1)} collective-permute-done((bf16[8,16,256]{2,1,0:T(8,128)(2,1)S(1)}, bf16[8,16,256]{2,1,0:T(8,128)(2,1)S(1)}, u32[]{:S(2)}, u32[]{:S(2)}) %collective-permute-start.7) | collective-permute-done | bytes 65568 | tf_op jit(solution)/shard_map/ppermute | solution.py:307
  107.2 1.3 %collective-permute-done.8.refs_3_ = bf16[8,16,256]{2,1,0:T(8,128)(2,1)S(1)} collective-permute-done((bf16[8,16,256]{2,1,0:T(8,128)(2,1)S(1)}, bf16[8,16,256]{2,1,0:T(8,128)(2,1)S(1)}, u32[]{:S(2)}, u32[]{:S(2)}) %collective-permute-start.8) | collective-permute-done | bytes 65568 | tf_op jit(solution)/shard_map/ppermute | solution.py:307
  108.6 1.6 %collective-permute-start.9 = (bf16[4,16,256]{2,1,0:T(8,128)(2,1)S(1)}, bf16[4,16,256]{2,1,0:T(8,128)(2,1)S(1)}, u32[]{:S(2)}, u32[]{:S(2)}) collective-permute-start(bf16[4,16,256]{2,1,0:T(8,128)(2,1)S(1)} %get-tuple-element.40), channel_id=1, source_target_pairs={{0,14},{1,15},{2,12},{3,13},{4,10},{5,11},{6,8},{7,9},{8,6},{9,7},... | collective-permute-start | bytes 98312 | tf_op jit(solution)/shard_map/ppermute | solution.py:307
  110.2 3.6 %collective-permute-done.9.refs_1_ = bf16[4,16,256]{2,1,0:T(8,128)(2,1)S(1)} collective-permute-done((bf16[4,16,256]{2,1,0:T(8,128)(2,1)S(1)}, bf16[4,16,256]{2,1,0:T(8,128)(2,1)S(1)}, u32[]{:S(2)}, u32[]{:S(2)}) %collective-permute-start.9) | collective-permute-done | bytes 32800 | tf_op jit(solution)/shard_map/ppermute | solution.py:307
  113.8 2.5 %collective-permute-start.10 = (bf16[2,16,256]{2,1,0:T(8,128)(2,1)S(1)}, bf16[2,16,256]{2,1,0:T(8,128)(2,1)S(1)}, u32[]{:S(2)}, u32[]{:S(2)}) collective-permute-start(bf16[2,16,256]{2,1,0:T(8,128)(2,1)S(1)} %get-tuple-element.42), channel_id=1, source_target_pairs={{0,4},{1,5},{2,6},{3,7},{4,0},{5,1},{6,2},{7,3},{8,12},{9,13},{10,... | collective-permute-start | bytes 49160 | tf_op jit(solution)/shard_map/ppermute | solution.py:307
  116.3 2.2 %collective-permute-done.10.refs_1_ = bf16[2,16,256]{2,1,0:T(8,128)(2,1)S(1)} collective-permute-done((bf16[2,16,256]{2,1,0:T(8,128)(2,1)S(1)}, bf16[2,16,256]{2,1,0:T(8,128)(2,1)S(1)}, u32[]{:S(2)}, u32[]{:S(2)}) %collective-permute-start.10) | collective-permute-done | bytes 16416 | tf_op jit(solution)/shard_map/ppermute | solution.py:307
  118.5 2.3 %collective-permute-start.11 = (bf16[1,16,256]{2,1,0:T(8,128)(2,1)S(1)}, bf16[1,16,256]{2,1,0:T(8,128)(2,1)S(1)}, u32[]{:S(2)}, u32[]{:S(2)}) collective-permute-start(bf16[1,16,256]{2,1,0:T(8,128)(2,1)S(1)} %get-tuple-element.44), channel_id=1, source_target_pairs={{0,2},{1,3},{2,0},{3,1},{4,6},{5,7},{6,4},{7,5},{8,10},{9,11},{10,... | collective-permute-start | bytes 24584 | tf_op jit(solution)/shard_map/ppermute | solution.py:307
  120.8 1.6 %collective-permute-done.11.refs_1_ = bf16[1,16,256]{2,1,0:T(8,128)(2,1)S(1)} collective-permute-done((bf16[1,16,256]{2,1,0:T(8,128)(2,1)S(1)}, bf16[1,16,256]{2,1,0:T(8,128)(2,1)S(1)}, u32[]{:S(2)}, u32[]{:S(2)}) %collective-permute-start.11) | collective-permute-done | bytes 8224 | tf_op jit(solution)/shard_map/ppermute | solution.py:307
  122.4 0.6 add.11
  (19 shorter events, 0.1 us)
Async XLA Ops:
  0.6 31.0 %copy-start = (bf16[256,256]{1,0:T(8,128)(2,1)S(1)}, bf16[256,256]{1,0:T(8,128)(2,1)}, u32[]{:S(2)}) copy-start(bf16[256,256]{1,0:T(8,128)(2,1)} %constant.6.clone.eye_ref) | copy-start | bytes 393220
  0.6 31.0 %copy-start.5 = (bf16[64,128]{1,0:T(8,128)(2,1)S(1)}, bf16[64,128]{1,0:T(8,128)(2,1)}, u32[]{:S(2)}) copy-start(bf16[64,128]{1,0:T(8,128)(2,1)} %constant.8.clone.pick_sum_ref) | copy-start | bytes 49156
  0.7 31.0 %copy-start.6 = (bf16[64,128]{1,0:T(8,128)(2,1)S(1)}, bf16[64,128]{1,0:T(8,128)(2,1)}, u32[]{:S(2)}) copy-start(bf16[64,128]{1,0:T(8,128)(2,1)} %constant.7.clone.pick_ref) | copy-start | bytes 49156
  0.7 31.0 %copy-start.4 = (s32[1,15360]{1,0:T(1,128)S(1)}, s32[1,15360]{1,0:T(1,128)}, u32[]{:S(2)}) copy-start(s32[1,15360]{1,0:T(1,128)} %coarse_codes_ref.1) | copy-start | bytes 184324
  0.7 31.0 %copy-start.3 = (s32[32,480]{1,0:T(8,128)S(1)}, s32[32,480]{1,0:T(8,128)}, u32[]{:S(2)}) copy-start(s32[32,480]{1,0:T(8,128)} %fine_codes_ref.1) | copy-start | bytes 184324
  0.7 31.0 %copy-start.7 = (bf16[16,144]{1,0:T(8,128)(2,1)S(1)}, bf16[16,144]{1,0:T(8,128)(2,1)}, u32[]{:S(2)}) copy-start(bf16[16,144]{1,0:T(8,128)(2,1)} %weights_ref.1) | copy-start | bytes 13828
  3.2 28.5 %copy-start.1 = (bf16[32,16,256]{2,1,0:T(8,128)(2,1)S(1)}, bf16[32,16,256]{2,1,0:T(8,128)(2,1)}, u32[]{:S(2)}) copy-start(bf16[32,16,256]{2,1,0:T(8,128)(2,1)} %get-tuple-element.25.head_ref) | copy-start | bytes 786436
  3.2 28.5 %copy-start.2 = (bf16[32,16,256]{2,1,0:T(8,128)(2,1)S(1)}, bf16[32,16,256]{2,1,0:T(8,128)(2,1)}, u32[]{:S(2)}) copy-start(bf16[32,16,256]{2,1,0:T(8,128)(2,1)} %get-tuple-element.24.tail_ref) | copy-start | bytes 786436
  3.2 28.5 %all-to-all-start = ((bf16[32,16,480]{2,1,0:T(8,128)(2,1)}), bf16[32,16,480]{2,1,0:T(8,128)(2,1)S(1)}, u32[]{:S(2)}, u32[]{:S(2)}) async-start(bf16[32,16,480]{2,1,0:T(8,128)(2,1)} %get-tuple-element.26), calls=%async_computation | async-start | bytes 1048576 | tf_op jit(solution)/shard_map/all_to_all | solution.py:373
  13.2 10.9 %collective-permute-start = (bf16[32,16,256]{2,1,0:T(8,128)(2,1)}, bf16[32,16,256]{2,1,0:T(8,128)(2,1)S(1)}, u32[]{:S(2)}, u32[]{:S(2)}) collective-permute-start(bf16[32,16,256]{2,1,0:T(8,128)(2,1)} %get-tuple-element.24.tail_ref), channel_id=1, source_target_pairs={{0,1},{1,2},{2,3},{3,4},{4,5},{5,6},{6,7},{7,8},{8,9},{9,10},{10,1... | collective-permute-start | bytes 786440 | tf_op jit(solution)/shard_map/ppermute | solution.py:370
  15.4 8.7 %collective-permute-start.1 = (bf16[32,16,256]{2,1,0:T(8,128)(2,1)}, bf16[32,16,256]{2,1,0:T(8,128)(2,1)S(1)}, u32[]{:S(2)}, u32[]{:S(2)}) collective-permute-start(bf16[32,16,256]{2,1,0:T(8,128)(2,1)} %get-tuple-element.25.head_ref), channel_id=1, source_target_pairs={{1,0},{2,1},{3,2},{4,3},{5,4},{6,5},{7,6},{8,7},{9,8},{10,9},{11,1... | collective-permute-start | bytes 786440 | tf_op jit(solution)/shard_map/ppermute | solution.py:371
  85.0 2.7 %collective-permute-start.2 = (bf16[128,16,256]{2,1,0:T(8,128)(2,1)S(1)}, bf16[128,16,256]{2,1,0:T(8,128)(2,1)S(1)}, u32[]{:S(2)}, u32[]{:S(2)}) collective-permute-start(bf16[128,16,256]{2,1,0:T(8,128)(2,1)S(1)} %bitcast.4), channel_id=1, source_target_pairs={{0,1},{1,0},{2,3},{3,2},{4,5},{5,4},{6,7},{7,6},{8,9},{9,8},{10,11... | collective-permute-start | bytes 3145736 | tf_op jit(solution)/shard_map/ppermute | solution.py:307
  88.1 6.4 %collective-permute-start.3 = (bf16[32,16,256]{2,1,0:T(8,128)(2,1)S(1)}, bf16[32,16,256]{2,1,0:T(8,128)(2,1)S(1)}, u32[]{:S(2)}, u32[]{:S(2)}) collective-permute-start(bf16[32,16,256]{2,1,0:T(8,128)(2,1)S(1)} %get-tuple-element.32), channel_id=1, source_target_pairs={{0,64},{1,17},{2,66},{3,19},{4,68},{5,21},{6,70},{7,23},{8,72},{9,... | collective-permute-start | bytes 786440 | tf_op jit(solution)/shard_map/ppermute | solution.py:307
  89.7 8.0 %collective-permute-start.4 = (bf16[32,16,256]{2,1,0:T(8,128)(2,1)S(1)}, bf16[32,16,256]{2,1,0:T(8,128)(2,1)S(1)}, u32[]{:S(2)}, u32[]{:S(2)}) collective-permute-start(bf16[32,16,256]{2,1,0:T(8,128)(2,1)S(1)} %get-tuple-element.33), channel_id=1, source_target_pairs={{0,128},{1,33},{2,130},{3,35},{4,132},{5,37},{6,134},{7,39},{8,136... | collective-permute-start | bytes 786440 | tf_op jit(solution)/shard_map/ppermute | solution.py:307
  90.8 9.2 %collective-permute-start.5 = (bf16[32,16,256]{2,1,0:T(8,128)(2,1)S(1)}, bf16[32,16,256]{2,1,0:T(8,128)(2,1)S(1)}, u32[]{:S(2)}, u32[]{:S(2)}) collective-permute-start(bf16[32,16,256]{2,1,0:T(8,128)(2,1)S(1)} %get-tuple-element.34), channel_id=1, source_target_pairs={{0,192},{1,49},{2,194},{3,51},{4,196},{5,53},{6,198},{7,55},{8,200... | collective-permute-start | bytes 786440 | tf_op jit(solution)/shard_map/ppermute | solution.py:307
  100.1 5.6 %collective-permute-start.6 = (bf16[8,16,256]{2,1,0:T(8,128)(2,1)S(1)}, bf16[8,16,256]{2,1,0:T(8,128)(2,1)S(1)}, u32[]{:S(2)}, u32[]{:S(2)}) collective-permute-start(bf16[8,16,256]{2,1,0:T(8,128)(2,1)S(1)} %get-tuple-element.36), channel_id=1, source_target_pairs={{0,16},{1,65},{2,18},{3,67},{4,20},{5,69},{6,22},{7,71},{8,24},{9,... | collective-permute-start | bytes 196616 | tf_op jit(solution)/shard_map/ppermute | solution.py:307
  101.4 5.8 %collective-permute-start.7 = (bf16[8,16,256]{2,1,0:T(8,128)(2,1)S(1)}, bf16[8,16,256]{2,1,0:T(8,128)(2,1)S(1)}, u32[]{:S(2)}, u32[]{:S(2)}) collective-permute-start(bf16[8,16,256]{2,1,0:T(8,128)(2,1)S(1)} %get-tuple-element.37), channel_id=1, source_target_pairs={{0,32},{1,129},{2,34},{3,131},{4,36},{5,133},{6,38},{7,135},{8,40}... | collective-permute-start | bytes 196616 | tf_op jit(solution)/shard_map/ppermute | solution.py:307
  104.3 4.3 %collective-permute-start.8 = (bf16[8,16,256]{2,1,0:T(8,128)(2,1)S(1)}, bf16[8,16,256]{2,1,0:T(8,128)(2,1)S(1)}, u32[]{:S(2)}, u32[]{:S(2)}) collective-permute-start(bf16[8,16,256]{2,1,0:T(8,128)(2,1)S(1)} %get-tuple-element.38), channel_id=1, source_target_pairs={{0,48},{1,193},{2,50},{3,195},{4,52},{5,197},{6,54},{7,199},{8,56}... | collective-permute-start | bytes 196616 | tf_op jit(solution)/shard_map/ppermute | solution.py:307
  108.6 5.2 %collective-permute-start.9 = (bf16[4,16,256]{2,1,0:T(8,128)(2,1)S(1)}, bf16[4,16,256]{2,1,0:T(8,128)(2,1)S(1)}, u32[]{:S(2)}, u32[]{:S(2)}) collective-permute-start(bf16[4,16,256]{2,1,0:T(8,128)(2,1)S(1)} %get-tuple-element.40), channel_id=1, source_target_pairs={{0,14},{1,15},{2,12},{3,13},{4,10},{5,11},{6,8},{7,9},{8,6},{9,7},... | collective-permute-start | bytes 98312 | tf_op jit(solution)/shard_map/ppermute | solution.py:307
  113.8 4.7 %collective-permute-start.10 = (bf16[2,16,256]{2,1,0:T(8,128)(2,1)S(1)}, bf16[2,16,256]{2,1,0:T(8,128)(2,1)S(1)}, u32[]{:S(2)}, u32[]{:S(2)}) collective-permute-start(bf16[2,16,256]{2,1,0:T(8,128)(2,1)S(1)} %get-tuple-element.42), channel_id=1, source_target_pairs={{0,4},{1,5},{2,6},{3,7},{4,0},{5,1},{6,2},{7,3},{8,12},{9,13},{10,... | collective-permute-start | bytes 49160 | tf_op jit(solution)/shard_map/ppermute | solution.py:307
  118.5 3.9 %collective-permute-start.11 = (bf16[1,16,256]{2,1,0:T(8,128)(2,1)S(1)}, bf16[1,16,256]{2,1,0:T(8,128)(2,1)S(1)}, u32[]{:S(2)}, u32[]{:S(2)}) collective-permute-start(bf16[1,16,256]{2,1,0:T(8,128)(2,1)S(1)} %get-tuple-element.44), channel_id=1, source_target_pairs={{0,2},{1,3},{2,0},{3,1},{4,6},{5,7},{6,4},{7,5},{8,10},{9,11},{10,... | collective-permute-start | bytes 24584 | tf_op jit(solution)/shard_map/ppermute | solution.py:307

commit v3 on v2

--- a/solution.py
+++ b/solution.py
@@ -165,10 +165,10 @@
             rows = [tables[k % TABLES][at[k], :] for k in range(8)]
             for k in range(8):
                 pltpu.store(tables[k % TABLES].at[at[k], :], rows[k] + tile, mask=sub == k)
-            out = rows[0]
-            for k in range(1, 8):
-                out = jnp.where(sub == k, rows[k], out)
-            vals_ref[here, :] = out
+            out = rows
+            for bit in (1, 2, 4):
+                out = [jnp.where((sub & bit) != 0, b, a) for a, b in zip(out[::2], out[1::2])]
+            vals_ref[here, :] = out[0]
 
     def step(i, carry):
         one(start + 2 * i)
@@ -253,8 +253,9 @@
     my_x, my_y, my_z, my_core = (lax.axis_index(a) for a in ("x", Y, "z", "core"))
 
     def total(i, carry):
-        for out_ref, core in ((send_ref, 1 - my_core), (keep_ref, my_core)):
-            b = 2 * i + core
+        for n, out_ref, core in ((0, send_ref, 1 - my_core), (0, keep_ref, my_core),
+                                 (1, send_ref, 1 - my_core), (1, keep_ref, my_core)):
+            b = 4 * i + 2 * n + core
             at = pl.ds(pl.multiple_of(b * 256 + 8, 8), 256)
             summed = t0[at, :] + t1[at, :] + t2[at, :] + t3[at, :]
             parts = nt(pick_sum, summed.astype(bf16)).astype(bf16)
@@ -268,7 +269,7 @@
                 out_ref[place] = parts[s * 16 : (s + 1) * 16]
         return carry
 
-    lax.fori_loop(0, ROWS // 512, total, 0)
+    lax.fori_loop(0, ROWS // 1024, total, 0)
     for q in range(LINES // 4):
         parts = []
         for k in range(4):
@@ -356,7 +357,7 @@
     keep, send = (v.reshape(128, CHANNELS, 256) for v in (keep, send))
     own, *sends = added(4, keep, permuted(send, lambda x, y, z, c: (x, y, z, 1 - c)))
     for first in (True, False):
-        got = [permuted(s, along(first, k + 1)) for k, s in enumerate(sends)]
+        got = [permuted(sends[k - 1], along(first, k)) for k in (2, 1, 3)]
         own, *sends = added(4 if first else 2, own, *got)
     for bits, ways in ((7, 2), (2, 2), (1, 1)):
         own, *sends = added(ways, own, permuted(sends[0], across(bits)))

time: 124 us -> 121 us (0.976)
  Pallas kernels: 64.3 us -> 61.5 us
    pallas_call x1, Pallas kernels: 53.2 us -> 50.5 us  [quantize(): pl.pallas_call(quantize_kernel, out_shape=[jax.ShapeDtypeStruct((LINES, C...]
  transfers between devices with their start and end apart: 13 -> 13, of which waited for: 10 -> 8; matrix products, arithmetic and copies ran while one was open for 0% -> 0% of each run, Pallas kernels for 6% -> 6%
where the time goes in v3:
time: 121 us; the launch traced here: 120 us
  Pallas kernels  61.5 us (51%)
  starting transfers between devices  30.6 us (25%)
  waiting for transfers between devices  27.2 us (22%)
    pallas_call x1, Pallas kernels, quantize(): pl.pallas_call(quantize_kernel, out_shape=[jax.ShapeDtypeStruct((LINES, C...  50.5 us
    ppermute x10, waiting for transfers between devices, permuted(): return lax.ppermute(value, CORES, pairs)  19.6 us
    ppermute x10, starting transfers between devices, permuted(): return lax.ppermute(value, CORES, pairs)  17.1 us
    all_to_all x1, starting transfers between devices, shards(): lax.all_to_all(lifted, SPACE, split_axis=0, concat_axis=0, tiled=True)  10 us
    all_to_all x1, waiting for transfers between devices, shards(): lax.all_to_all(lifted, SPACE, split_axis=0, concat_axis=0, tiled=True)  7.55 us
    pallas_call x1, Pallas kernels, code_table(): pl.pallas_call(table_kernel, grid=(ROWS // 2048,), out_shape=jax.ShapeDty...  7.39 us
    pallas_call x1, Pallas kernels, lift(): pl.pallas_call(lift_kernel, out_shape=[edge, edge, shape], grid=(2,), in_...  2.48 us
  transfers between devices with their start and end apart: 13, of which 8 were waited for; matrix products, arithmetic and copies ran while one was open for 0% of the time, Pallas kernels for 6%

profile of v3, /device:TPU:2, one launch (start us, length us, event | category | flops | bytes accessed | tf_op | source)
XLA Modules:
  0.0 120.2 jit_solution(1429492906651935428)
XLA Ops:
  0.6 0.0 copy-start
  0.6 0.0 copy-start.5
  0.7 0.0 copy-start.6
  0.7 2.5 %lift.1 = (bf16[32,16,256]{2,1,0:T(8,128)(2,1)}, bf16[32,16,256]{2,1,0:T(8,128)(2,1)}, bf16[32,16,480]{2,1,0:T(8,128)(2,1)}) custom-call(bf16[64,16,480]{2,1,0:T(8,128)(2,1)} %lat_ref.1), custom_call_target="tpu_custom_call" | custom-call | tf_op jit(solution)/shard_map/lift/pallas_call | solution.py:68
  3.2 10.0 %all-to-all-start = ((bf16[32,16,480]{2,1,0:T(8,128)(2,1)}), bf16[32,16,480]{2,1,0:T(8,128)(2,1)S(1)}, u32[]{:S(2)}, u32[]{:S(2)}) async-start(bf16[32,16,480]{2,1,0:T(8,128)(2,1)} %get-tuple-element.26), calls=%async_computation | async-start | bytes 1048576 | tf_op jit(solution)/shard_map/all_to_all | solution.py:374
  13.2 2.2 %collective-permute-start = (bf16[32,16,256]{2,1,0:T(8,128)(2,1)}, bf16[32,16,256]{2,1,0:T(8,128)(2,1)S(1)}, u32[]{:S(2)}, u32[]{:S(2)}) collective-permute-start(bf16[32,16,256]{2,1,0:T(8,128)(2,1)} %get-tuple-element.24.tail_ref), channel_id=1, source_target_pairs={{0,1},{1,2},{2,3},{3,4},{4,5},{5,6},{6,7},{7,8},{8,9},{9,10},{10,1... | collective-permute-start | bytes 786440 | tf_op jit(solution)/shard_map/ppermute | solution.py:371
  15.4 1.3 %collective-permute-start.1 = (bf16[32,16,256]{2,1,0:T(8,128)(2,1)}, bf16[32,16,256]{2,1,0:T(8,128)(2,1)S(1)}, u32[]{:S(2)}, u32[]{:S(2)}) collective-permute-start(bf16[32,16,256]{2,1,0:T(8,128)(2,1)} %get-tuple-element.25.head_ref), channel_id=1, source_target_pairs={{1,0},{2,1},{3,2},{4,3},{5,4},{6,5},{7,6},{8,7},{9,8},{10,9},{11,1... | collective-permute-start | bytes 786440 | tf_op jit(solution)/shard_map/ppermute | solution.py:372
  16.7 7.4 %code_table.1.table_in = f32[16384,128]{1,0:T(8,128)} custom-call(bf16[16,65536]{1,0:T(8,128)(2,1)} %codebook_ref.1, bf16[256,256]{1,0:T(8,128)(2,1)} %constant.6.clone.eye_ref), custom_call_target="tpu_custom_call" | custom-call | flops 1000000000 | bytes 10000000 | tf_op jit(solution)/shard_map/code_table/pallas_call | solution.py:97
  24.1 0.0 collective-permute-done.before_ref
  24.1 0.0 collective-permute-done.1.after_ref
  24.1 7.5 %all-to-all-done.values_ref = bf16[32,16,480]{2,1,0:T(8,128)(2,1)S(1)} async-done(((bf16[32,16,480]{2,1,0:T(8,128)(2,1)}), bf16[32,16,480]{2,1,0:T(8,128)(2,1)S(1)}, u32[]{:S(2)}, u32[]{:S(2)}) %all-to-all-start) | async-done | bytes 491552 | tf_op jit(solution)/shard_map/all_to_all | solution.py:374
  31.7 50.5 %quantize.1 = (bf16[32,16,480]{2,1,0:T(8,128)(2,1)}, bf16[1,16,15360]{2,1,0:T(8,128)(2,1)}, bf16[4,4,8,16,256]{4,3,2,1,0:T(8,128)(2,1)S(1)}, bf16[4,4,8,16,256]{4,3,2,1,0:T(8,128)(2,1)S(1)}) custom-call(bf16[32,16,256]{2,1,0:T(8,128)(2,1)S(1)} %collective-permute-done.before_ref, bf16[32,16,256]{2,1,0:T(8,128)(2,1)S(1)} %copy-done.1, ...), custom_call_target="tpu_custom_call" | custom-call | flops 1000000000 | bytes 100000000 | tf_op jit(solution)/shard_map/quantize/pallas_call | solution.py:284
  82.2 0.1 collective-permute-start.2
  82.3 2.6 %collective-permute-done.2.refs_1_ = bf16[128,16,256]{2,1,0:T(8,128)(2,1)S(1)} collective-permute-done((bf16[128,16,256]{2,1,0:T(8,128)(2,1)S(1)}, bf16[128,16,256]{2,1,0:T(8,128)(2,1)S(1)}, u32[]{:S(2)}, u32[]{:S(2)}) %collective-permute-start.2) | collective-permute-done | bytes 1048608 | tf_op jit(solution)/shard_map/ppermute | solution.py:308
  84.9 0.4 add.6
  85.3 2.2 %collective-permute-start.3 = (bf16[32,16,256]{2,1,0:T(8,128)(2,1)S(1)}, bf16[32,16,256]{2,1,0:T(8,128)(2,1)S(1)}, u32[]{:S(2)}, u32[]{:S(2)}) collective-permute-start(bf16[32,16,256]{2,1,0:T(8,128)(2,1)S(1)} %get-tuple-element.32), channel_id=1, source_target_pairs={{0,128},{1,33},{2,130},{3,35},{4,132},{5,37},{6,134},{7,39},{8,136... | collective-permute-start | bytes 786440 | tf_op jit(solution)/shard_map/ppermute | solution.py:308
  87.5 2.0 %collective-permute-start.5 = (bf16[32,16,256]{2,1,0:T(8,128)(2,1)S(1)}, bf16[32,16,256]{2,1,0:T(8,128)(2,1)S(1)}, u32[]{:S(2)}, u32[]{:S(2)}) collective-permute-start(bf16[32,16,256]{2,1,0:T(8,128)(2,1)S(1)} %get-tuple-element.34), channel_id=1, source_target_pairs={{0,192},{1,49},{2,194},{3,51},{4,196},{5,53},{6,198},{7,55},{8,200... | collective-permute-start | bytes 786440 | tf_op jit(solution)/shard_map/ppermute | solution.py:308
  89.5 3.8 %collective-permute-done.3.refs_1_ = bf16[32,16,256]{2,1,0:T(8,128)(2,1)S(1)} collective-permute-done((bf16[32,16,256]{2,1,0:T(8,128)(2,1)S(1)}, bf16[32,16,256]{2,1,0:T(8,128)(2,1)S(1)}, u32[]{:S(2)}, u32[]{:S(2)}) %collective-permute-start.3) | collective-permute-done | bytes 262176 | tf_op jit(solution)/shard_map/ppermute | solution.py:308
  93.4 2.8 %collective-permute-done.4.refs_2_ = bf16[32,16,256]{2,1,0:T(8,128)(2,1)S(1)} collective-permute-done((bf16[32,16,256]{2,1,0:T(8,128)(2,1)S(1)}, bf16[32,16,256]{2,1,0:T(8,128)(2,1)S(1)}, u32[]{:S(2)}, u32[]{:S(2)}) %collective-permute-start.4) | collective-permute-done | bytes 262176 | tf_op jit(solution)/shard_map/ppermute | solution.py:308
  96.1 0.0 collective-permute-done.5.refs_3_
  96.2 0.1 add.7
  96.3 3.0 %collective-permute-start.6 = (bf16[8,16,256]{2,1,0:T(8,128)(2,1)S(1)}, bf16[8,16,256]{2,1,0:T(8,128)(2,1)S(1)}, u32[]{:S(2)}, u32[]{:S(2)}) collective-permute-start(bf16[8,16,256]{2,1,0:T(8,128)(2,1)S(1)} %get-tuple-element.36), channel_id=1, source_target_pairs={{0,32},{1,129},{2,34},{3,131},{4,36},{5,133},{6,38},{7,135},{8,40}... | collective-permute-start | bytes 196616 | tf_op jit(solution)/shard_map/ppermute | solution.py:308
  99.3 0.6 collective-permute-start.7
  99.9 2.7 %collective-permute-start.8 = (bf16[8,16,256]{2,1,0:T(8,128)(2,1)S(1)}, bf16[8,16,256]{2,1,0:T(8,128)(2,1)S(1)}, u32[]{:S(2)}, u32[]{:S(2)}) collective-permute-start(bf16[8,16,256]{2,1,0:T(8,128)(2,1)S(1)} %get-tuple-element.38), channel_id=1, source_target_pairs={{0,48},{1,193},{2,50},{3,195},{4,52},{5,197},{6,54},{7,199},{8,56}... | collective-permute-start | bytes 196616 | tf_op jit(solution)/shard_map/ppermute | solution.py:308
  102.5 2.2 %collective-permute-done.7.refs_2_ = bf16[8,16,256]{2,1,0:T(8,128)(2,1)S(1)} collective-permute-done((bf16[8,16,256]{2,1,0:T(8,128)(2,1)S(1)}, bf16[8,16,256]{2,1,0:T(8,128)(2,1)S(1)}, u32[]{:S(2)}, u32[]{:S(2)}) %collective-permute-start.7) | collective-permute-done | bytes 65568 | tf_op jit(solution)/shard_map/ppermute | solution.py:308
  104.8 1.3 %collective-permute-start.9 = (bf16[4,16,256]{2,1,0:T(8,128)(2,1)S(1)}, bf16[4,16,256]{2,1,0:T(8,128)(2,1)S(1)}, u32[]{:S(2)}, u32[]{:S(2)}) collective-permute-start(bf16[4,16,256]{2,1,0:T(8,128)(2,1)S(1)} %get-tuple-element.40), channel_id=1, source_target_pairs={{0,14},{1,15},{2,12},{3,13},{4,10},{5,11},{6,8},{7,9},{8,6},{9,7},... | collective-permute-start | bytes 98312 | tf_op jit(solution)/shard_map/ppermute | solution.py:308
  106.1 3.9 %collective-permute-done.9.refs_1_ = bf16[4,16,256]{2,1,0:T(8,128)(2,1)S(1)} collective-permute-done((bf16[4,16,256]{2,1,0:T(8,128)(2,1)S(1)}, bf16[4,16,256]{2,1,0:T(8,128)(2,1)S(1)}, u32[]{:S(2)}, u32[]{:S(2)}) %collective-permute-start.9) | collective-permute-done | bytes 32800 | tf_op jit(solution)/shard_map/ppermute | solution.py:308
  110.0 2.2 %collective-permute-start.10 = (bf16[2,16,256]{2,1,0:T(8,128)(2,1)S(1)}, bf16[2,16,256]{2,1,0:T(8,128)(2,1)S(1)}, u32[]{:S(2)}, u32[]{:S(2)}) collective-permute-start(bf16[2,16,256]{2,1,0:T(8,128)(2,1)S(1)} %get-tuple-element.42), channel_id=1, source_target_pairs={{0,4},{1,5},{2,6},{3,7},{4,0},{5,1},{6,2},{7,3},{8,12},{9,13},{10,... | collective-permute-start | bytes 49160 | tf_op jit(solution)/shard_map/ppermute | solution.py:308
  112.2 2.5 %collective-permute-done.10.refs_1_ = bf16[2,16,256]{2,1,0:T(8,128)(2,1)S(1)} collective-permute-done((bf16[2,16,256]{2,1,0:T(8,128)(2,1)S(1)}, bf16[2,16,256]{2,1,0:T(8,128)(2,1)S(1)}, u32[]{:S(2)}, u32[]{:S(2)}) %collective-permute-start.10) | collective-permute-done | bytes 16416 | tf_op jit(solution)/shard_map/ppermute | solution.py:308
  114.8 3.1 %collective-permute-start.11 = (bf16[1,16,256]{2,1,0:T(8,128)(2,1)S(1)}, bf16[1,16,256]{2,1,0:T(8,128)(2,1)S(1)}, u32[]{:S(2)}, u32[]{:S(2)}) collective-permute-start(bf16[1,16,256]{2,1,0:T(8,128)(2,1)S(1)} %get-tuple-element.44), channel_id=1, source_target_pairs={{0,2},{1,3},{2,0},{3,1},{4,6},{5,7},{6,4},{7,5},{8,10},{9,11},{10,... | collective-permute-start | bytes 24584 | tf_op jit(solution)/shard_map/ppermute | solution.py:308
  117.9 1.6 %collective-permute-done.11.refs_1_ = bf16[1,16,256]{2,1,0:T(8,128)(2,1)S(1)} collective-permute-done((bf16[1,16,256]{2,1,0:T(8,128)(2,1)S(1)}, bf16[1,16,256]{2,1,0:T(8,128)(2,1)S(1)}, u32[]{:S(2)}, u32[]{:S(2)}) %collective-permute-start.11) | collective-permute-done | bytes 8224 | tf_op jit(solution)/shard_map/ppermute | solution.py:308
  119.5 0.6 add.11
  (19 shorter events, 0.1 us)
Async XLA Ops:
  0.6 31.0 %copy-start = (bf16[256,256]{1,0:T(8,128)(2,1)S(1)}, bf16[256,256]{1,0:T(8,128)(2,1)}, u32[]{:S(2)}) copy-start(bf16[256,256]{1,0:T(8,128)(2,1)} %constant.6.clone.eye_ref) | copy-start | bytes 393220
  0.6 31.0 %copy-start.5 = (bf16[64,128]{1,0:T(8,128)(2,1)S(1)}, bf16[64,128]{1,0:T(8,128)(2,1)}, u32[]{:S(2)}) copy-start(bf16[64,128]{1,0:T(8,128)(2,1)} %constant.8.clone.pick_sum_ref) | copy-start | bytes 49156
  0.7 31.0 %copy-start.6 = (bf16[64,128]{1,0:T(8,128)(2,1)S(1)}, bf16[64,128]{1,0:T(8,128)(2,1)}, u32[]{:S(2)}) copy-start(bf16[64,128]{1,0:T(8,128)(2,1)} %constant.7.clone.pick_ref) | copy-start | bytes 49156
  0.7 31.0 %copy-start.4 = (s32[1,15360]{1,0:T(1,128)S(1)}, s32[1,15360]{1,0:T(1,128)}, u32[]{:S(2)}) copy-start(s32[1,15360]{1,0:T(1,128)} %coarse_codes_ref.1) | copy-start | bytes 184324
  0.7 31.0 %copy-start.3 = (s32[32,480]{1,0:T(8,128)S(1)}, s32[32,480]{1,0:T(8,128)}, u32[]{:S(2)}) copy-start(s32[32,480]{1,0:T(8,128)} %fine_codes_ref.1) | copy-start | bytes 184324
  0.7 31.0 %copy-start.7 = (bf16[16,144]{1,0:T(8,128)(2,1)S(1)}, bf16[16,144]{1,0:T(8,128)(2,1)}, u32[]{:S(2)}) copy-start(bf16[16,144]{1,0:T(8,128)(2,1)} %weights_ref.1) | copy-start | bytes 13828
  3.2 28.5 %copy-start.1 = (bf16[32,16,256]{2,1,0:T(8,128)(2,1)S(1)}, bf16[32,16,256]{2,1,0:T(8,128)(2,1)}, u32[]{:S(2)}) copy-start(bf16[32,16,256]{2,1,0:T(8,128)(2,1)} %get-tuple-element.25.head_ref) | copy-start | bytes 786436
  3.2 28.5 %copy-start.2 = (bf16[32,16,256]{2,1,0:T(8,128)(2,1)S(1)}, bf16[32,16,256]{2,1,0:T(8,128)(2,1)}, u32[]{:S(2)}) copy-start(bf16[32,16,256]{2,1,0:T(8,128)(2,1)} %get-tuple-element.24.tail_ref) | copy-start | bytes 786436
  3.2 28.5 %all-to-all-start = ((bf16[32,16,480]{2,1,0:T(8,128)(2,1)}), bf16[32,16,480]{2,1,0:T(8,128)(2,1)S(1)}, u32[]{:S(2)}, u32[]{:S(2)}) async-start(bf16[32,16,480]{2,1,0:T(8,128)(2,1)} %get-tuple-element.26), calls=%async_computation | async-start | bytes 1048576 | tf_op jit(solution)/shard_map/all_to_all | solution.py:374
  13.2 10.9 %collective-permute-start = (bf16[32,16,256]{2,1,0:T(8,128)(2,1)}, bf16[32,16,256]{2,1,0:T(8,128)(2,1)S(1)}, u32[]{:S(2)}, u32[]{:S(2)}) collective-permute-start(bf16[32,16,256]{2,1,0:T(8,128)(2,1)} %get-tuple-element.24.tail_ref), channel_id=1, source_target_pairs={{0,1},{1,2},{2,3},{3,4},{4,5},{5,6},{6,7},{7,8},{8,9},{9,10},{10,1... | collective-permute-start | bytes 786440 | tf_op jit(solution)/shard_map/ppermute | solution.py:371
  15.4 8.7 %collective-permute-start.1 = (bf16[32,16,256]{2,1,0:T(8,128)(2,1)}, bf16[32,16,256]{2,1,0:T(8,128)(2,1)S(1)}, u32[]{:S(2)}, u32[]{:S(2)}) collective-permute-start(bf16[32,16,256]{2,1,0:T(8,128)(2,1)} %get-tuple-element.25.head_ref), channel_id=1, source_target_pairs={{1,0},{2,1},{3,2},{4,3},{5,4},{6,5},{7,6},{8,7},{9,8},{10,9},{11,1... | collective-permute-start | bytes 786440 | tf_op jit(solution)/shard_map/ppermute | solution.py:372
  82.2 2.7 %collective-permute-start.2 = (bf16[128,16,256]{2,1,0:T(8,128)(2,1)S(1)}, bf16[128,16,256]{2,1,0:T(8,128)(2,1)S(1)}, u32[]{:S(2)}, u32[]{:S(2)}) collective-permute-start(bf16[128,16,256]{2,1,0:T(8,128)(2,1)S(1)} %bitcast.4), channel_id=1, source_target_pairs={{0,1},{1,0},{2,3},{3,2},{4,5},{5,4},{6,7},{7,6},{8,9},{9,8},{10,11... | collective-permute-start | bytes 3145736 | tf_op jit(solution)/shard_map/ppermute | solution.py:308
  85.3 8.1 %collective-permute-start.3 = (bf16[32,16,256]{2,1,0:T(8,128)(2,1)S(1)}, bf16[32,16,256]{2,1,0:T(8,128)(2,1)S(1)}, u32[]{:S(2)}, u32[]{:S(2)}) collective-permute-start(bf16[32,16,256]{2,1,0:T(8,128)(2,1)S(1)} %get-tuple-element.32), channel_id=1, source_target_pairs={{0,128},{1,33},{2,130},{3,35},{4,132},{5,37},{6,134},{7,39},{8,136... | collective-permute-start | bytes 786440 | tf_op jit(solution)/shard_map/ppermute | solution.py:308
  87.5 8.6 %collective-permute-start.4 = (bf16[32,16,256]{2,1,0:T(8,128)(2,1)S(1)}, bf16[32,16,256]{2,1,0:T(8,128)(2,1)S(1)}, u32[]{:S(2)}, u32[]{:S(2)}) collective-permute-start(bf16[32,16,256]{2,1,0:T(8,128)(2,1)S(1)} %get-tuple-element.33), channel_id=1, source_target_pairs={{0,64},{1,17},{2,66},{3,19},{4,68},{5,21},{6,70},{7,23},{8,72},{9,... | collective-permute-start | bytes 786440 | tf_op jit(solution)/shard_map/ppermute | solution.py:308
  87.5 8.6 %collective-permute-start.5 = (bf16[32,16,256]{2,1,0:T(8,128)(2,1)S(1)}, bf16[32,16,256]{2,1,0:T(8,128)(2,1)S(1)}, u32[]{:S(2)}, u32[]{:S(2)}) collective-permute-start(bf16[32,16,256]{2,1,0:T(8,128)(2,1)S(1)} %get-tuple-element.34), channel_id=1, source_target_pairs={{0,192},{1,49},{2,194},{3,51},{4,196},{5,53},{6,198},{7,55},{8,200... | collective-permute-start | bytes 786440 | tf_op jit(solution)/shard_map/ppermute | solution.py:308
  96.3 6.2 %collective-permute-start.6 = (bf16[8,16,256]{2,1,0:T(8,128)(2,1)S(1)}, bf16[8,16,256]{2,1,0:T(8,128)(2,1)S(1)}, u32[]{:S(2)}, u32[]{:S(2)}) collective-permute-start(bf16[8,16,256]{2,1,0:T(8,128)(2,1)S(1)} %get-tuple-element.36), channel_id=1, source_target_pairs={{0,32},{1,129},{2,34},{3,131},{4,36},{5,133},{6,38},{7,135},{8,40}... | collective-permute-start | bytes 196616 | tf_op jit(solution)/shard_map/ppermute | solution.py:308
  99.3 5.5 %collective-permute-start.7 = (bf16[8,16,256]{2,1,0:T(8,128)(2,1)S(1)}, bf16[8,16,256]{2,1,0:T(8,128)(2,1)S(1)}, u32[]{:S(2)}, u32[]{:S(2)}) collective-permute-start(bf16[8,16,256]{2,1,0:T(8,128)(2,1)S(1)} %get-tuple-element.37), channel_id=1, source_target_pairs={{0,16},{1,65},{2,18},{3,67},{4,20},{5,69},{6,22},{7,71},{8,24},{9,... | collective-permute-start | bytes 196616 | tf_op jit(solution)/shard_map/ppermute | solution.py:308
  99.9 4.9 %collective-permute-start.8 = (bf16[8,16,256]{2,1,0:T(8,128)(2,1)S(1)}, bf16[8,16,256]{2,1,0:T(8,128)(2,1)S(1)}, u32[]{:S(2)}, u32[]{:S(2)}) collective-permute-start(bf16[8,16,256]{2,1,0:T(8,128)(2,1)S(1)} %get-tuple-element.38), channel_id=1, source_target_pairs={{0,48},{1,193},{2,50},{3,195},{4,52},{5,197},{6,54},{7,199},{8,56}... | collective-permute-start | bytes 196616 | tf_op jit(solution)/shard_map/ppermute | solution.py:308
  104.8 5.2 %collective-permute-start.9 = (bf16[4,16,256]{2,1,0:T(8,128)(2,1)S(1)}, bf16[4,16,256]{2,1,0:T(8,128)(2,1)S(1)}, u32[]{:S(2)}, u32[]{:S(2)}) collective-permute-start(bf16[4,16,256]{2,1,0:T(8,128)(2,1)S(1)} %get-tuple-element.40), channel_id=1, source_target_pairs={{0,14},{1,15},{2,12},{3,13},{4,10},{5,11},{6,8},{7,9},{8,6},{9,7},... | collective-permute-start | bytes 98312 | tf_op jit(solution)/shard_map/ppermute | solution.py:308
  110.0 4.7 %collective-permute-start.10 = (bf16[2,16,256]{2,1,0:T(8,128)(2,1)S(1)}, bf16[2,16,256]{2,1,0:T(8,128)(2,1)S(1)}, u32[]{:S(2)}, u32[]{:S(2)}) collective-permute-start(bf16[2,16,256]{2,1,0:T(8,128)(2,1)S(1)} %get-tuple-element.42), channel_id=1, source_target_pairs={{0,4},{1,5},{2,6},{3,7},{4,0},{5,1},{6,2},{7,3},{8,12},{9,13},{10,... | collective-permute-start | bytes 49160 | tf_op jit(solution)/shard_map/ppermute | solution.py:308
  114.8 4.8 %collective-permute-start.11 = (bf16[1,16,256]{2,1,0:T(8,128)(2,1)S(1)}, bf16[1,16,256]{2,1,0:T(8,128)(2,1)S(1)}, u32[]{:S(2)}, u32[]{:S(2)}) collective-permute-start(bf16[1,16,256]{2,1,0:T(8,128)(2,1)S(1)} %get-tuple-element.44), channel_id=1, source_target_pairs={{0,2},{1,3},{2,0},{3,1},{4,6},{5,7},{6,4},{7,5},{8,10},{9,11},{10,... | collective-permute-start | bytes 24584 | tf_op jit(solution)/shard_map/ppermute | solution.py:308
